TPU v7x, 512 devices: a whole 4x8x8 slice. The times are simulated.
512 devices in a mesh: rep: 8 (over x, core), dp: 8 (over z), expert: 8 (over y).
Axes of the slice: x: 4, y: 8, z: 8, core: 2. Of those that a mesh axis runs over, the one named last changes fastest.
Arguments:
- layer_out: bfloat16 [8192, 4096], P(('dp', 'expert'), 'rep'), may hold values from -6 to 6
- frozen_out: bfloat16 [8192, 4096], P(('dp', 'expert'), 'rep'), may hold values from -6 to 6
- control: float32 [4096], P('rep'), may hold values from -6 to 6
- row_kind: int32 [8192], P(('dp', 'expert')), may hold values 0 or 1
- expert_ids: int32 [8192, 2], P(('dp', 'expert')), may hold values from 0 to 7, all different within a row; in each aligned block of 128 rows (0 to 127, 128 to 255, ...) at most 48 rows name the same one
- route_weights: float32 [8192, 2], P(('dp', 'expert')), may hold values from 0.2 to 1
- hidden: bfloat16 [8, 3072, 14336], P('expert', 'rep', 'dp'), may hold values from -6 to 6
Outputs:
- grad_down: float32 [8, 14336, 4096], P('expert', 'dp', 'rep')
Inputs may be any that keep to these rules, and one draw needn't show every extreme that they name: `expert_ids`: each token names two different experts; among the 128 tokens of one index of dp and expert no expert is named more than 48 times, and in every draw some expert of some such block is named exactly 48 times.
All inputs are finite; a program needn't handle non-finite values. No bound on the sum of `row_kind` on one device may be relied on, other than what follows from the above.
Results may differ from a plain program's by a relative error of at most 0.0029.
Values may be sent and summed in bfloat16 or wider, within the bound.
No kernel may reach another device: no remote copies, remote signals or barrier semaphores. Data moves between devices by JAX's collectives and lax.ppermute only.
A program may use at most 64 MiB of HBM per device.

v0:
```python
import math

import jax
import jax.numpy as jnp
from jax import lax
from jax.sharding import PartitionSpec as P

retain_weight = 2.0


def spread(outgoing, dp_count):
    copies = jnp.broadcast_to(outgoing[None], (dp_count,) + outgoing.shape)
    copies = copies.reshape(dp_count * outgoing.shape[0], outgoing.shape[1], outgoing.shape[2])
    return lax.all_to_all(
        copies.astype(jnp.bfloat16), ("dp", "expert"), split_axis=0, concat_axis=1, tiled=True
    ).astype(copies.dtype)


def body(layer_out, frozen_out, control, row_kind, expert_ids, route_weights, hidden):
    tok_rows, feat_cols = layer_out.shape
    exp_local = hidden.shape[0]
    dp_count = lax.axis_size("dp")
    exp_count = lax.axis_size("expert")
    experts_all = exp_local * exp_count
    capacity = tok_rows * 3 // 8
    flat_ids = expert_ids.reshape(-1)
    matches = (flat_ids[:, None] == jnp.arange(experts_all, dtype=jnp.int32)[None, :]).astype(
        jnp.int32
    )
    before = jnp.cumsum(matches, axis=0) - matches
    slot_idx = jnp.sum(before * matches, axis=1)
    column_idx = flat_ids * capacity + slot_idx
    columns = jnp.arange(experts_all * capacity, dtype=jnp.int32)
    placed = (
        (column_idx[:, None] == columns[None, :])
        .astype(jnp.float32)
        .reshape(tok_rows, 2, experts_all * capacity)
    )
    weighted = jnp.sum(placed * route_weights[:, :, None], axis=1)
    retain = (row_kind == 1)[:, None]
    target = jnp.where(retain, frozen_out.astype(jnp.float32), control[None, :])
    row_scale = jnp.where(retain, jnp.float32(retain_weight), jnp.float32(1.0))
    total_tokens = tok_rows * dp_count * exp_count
    out_grad = (
        row_scale * (layer_out.astype(jnp.float32) - target) * (1.0 / math.sqrt(total_tokens))
    )
    grad_send = jnp.dot(weighted.T, out_grad, precision=lax.Precision.HIGHEST)
    grad_send = grad_send.reshape(experts_all, capacity, feat_cols)
    grad_rows = spread(grad_send, dp_count)
    grad_high = grad_rows.astype(jnp.bfloat16)
    return jnp.einsum(
        "jmf,jmd->jfd",
        lax.all_gather(hidden, "rep", axis=1, tiled=True),
        grad_high,
        preferred_element_type=jnp.float32,
    )


def solution(mesh):
    in_specs = (
        P(("dp", "expert"), "rep"),
        P(("dp", "expert"), "rep"),
        P("rep"),
        P(("dp", "expert")),
        P(("dp", "expert"), None),
        P(("dp", "expert"), None),
        P("expert", "rep", "dp"),
    )
    out_specs = P("expert", "dp", "rep")
    return jax.shard_map(body, mesh=mesh, in_specs=in_specs, out_specs=out_specs, check_vma=False)
```

profile of v0, /device:TPU:6, one launch (start us, length us, event | category | flops | bytes accessed | tf_op | source)
XLA Modules:
  0.0 128.3 jit_solution(13240547953223724485)
XLA Ops:
  6.5 0.0 all-gather.2.cloned.1.call-start
  6.5 0.7 all-gather.2.cloned.1.call-update
  7.3 0.8 copy.31
  8.0 0.1 eq.49
  8.2 0.1 eq.45
  8.3 0.6 reduce-window.6
  8.9 0.2 slice_reduce_fusion
  9.2 0.1 fusion.17
  9.3 0.1 reduce_sum.21
  9.4 0.1 copy.33
  9.5 0.7 multiply_add_fusion
  10.2 0.8 select_reduce_fusion
  11.0 0.1 copy.34
  11.2 0.7 broadcast_select_fusion
  11.8 0.7 broadcast_compare_fusion
  12.5 1.9 %convolution_convert_fusion = bf16[8,48,512]{2,1,0:T(8,128)(2,1)S(1)} fusion(f32[8,48,128]{2,1,0:T(8,128)S(1)} %bitcast.29, bf16[128,512]{1,0:T(8,128)(2,1)} %param.8, bf16[128,512]{1,0:T(8,128)(2,1)} %param.7, f32[512]{0:T(512)} %param.9, f32[128]{0:T(128)S(1)} %broadcast_select_fusion, pred[128]{0:T(512)(128)(4,1)S(1)} %broadcast_compare_fusion), kind=kOutput, calls=%fused_computation.3 | convolution fusion | flops 302579712 | bytes 854656 | tf_op jit(solution)/shard_map/dot_general | solution.py:47
  14.3 0.4 broadcast_in_dim.39
  14.7 91.0 %all_to_all.4 = bf16[64,48,512]{2,1,0:T(8,128)(2,1)S(1)} all-to-all(bf16[64,48,512]{2,1,0:T(8,128)(2,1)S(1)} %bitcast.26), channel_id=1, replica_groups=mesh['rep'=8,'dp'=8,'expert'=8] {'dp','expert'}, dimensions={0} | all-to-all | bytes 6291456 | tf_op jit(solution)/shard_map/all_to_all | solution.py:14
  105.8 0.0 all-gather.2.cloned.1.call-done
  105.8 10.6 %fusion.2 = f32[1,1792,512]{1,2,0:T(8,128)} fusion(bf16[3072,512]{1,0:T(8,128)(2,1)S(1)} %bitcast.27, bf16[1,3072,1792]{2,1,0:T(8,128)(2,1)} %all-gather.2.cloned.1.call-done), kind=kOutput, calls=%fused_computation.2 | convolution fusion | flops 5637144576 | bytes 17825792 | tf_op jit(solution)/shard_map/jmf,jmd->jfd/dot_general | solution.py:51
  116.4 5.1 %copy.35 = f32[1,1792,512]{2,1,0:T(8,128)} copy(f32[1,1792,512]{1,2,0:T(8,128)} %fusion.2) | data formatting | bytes 7340032 | tf_op jit(solution)/shard_map/jmf,jmd->jfd/dot_general | solution.py:51
  (3 shorter events, 0.0 us)
Async XLA Ops:
  6.5 99.2 %all-gather.2.cloned.1.call-start = ((), (), s32[]{:S(2)}) async-start(), calls=%async_computation.1 | async-start | bytes 12386304 | tf_op jit(solution)/shard_map/all_gather | solution.py:53
Sparse Core Ops, SparseCore 0:
  9.5 68.8 all-gather.1
where the time goes:
time: 129 us; the launch traced here: 128 us
  blocking collectives  91 us (71%)
  between operations  13.4 us (10%)
  matrix products  12.5 us (10%)
  local copies, waits for them, and re-layouts  7.09 us (5%)
  other arithmetic  3.57 us (3%)
    all_to_all x1, blocking collectives, spread(): lax.all_to_all(copies.astype(jnp.bfloat16), ('dp', 'expert'), split_axis=...  91 us
    dot_general x1, matrix products, body(): jnp.einsum('jmf,jmd->jfd', lax.all_gather(hidden, 'rep', axis=1, tiled=Tr...  10.6 us
    dot_general x1, local copies, waits for them, and re-layouts, body(): jnp.einsum('jmf,jmd->jfd', lax.all_gather(hidden, 'rep', axis=1, tiled=Tr...  5.11 us
  transfers between devices with their start and end apart: 1, of which 0 were waited for; matrix products, arithmetic and copies ran while one was open for 6% of the time, Pallas kernels for 0%

commit v1 on v0

v1 whole, which is shorter than its diff:
```python
import math

import jax
import jax.numpy as jnp
from jax import lax
from jax.experimental import pallas as pl
from jax.experimental.pallas import tpu as pltpu
from jax.sharding import PartitionSpec as P

retain_weight = 2.0
tile = 256
split = 768


def ring(count, step, stride=1):
    return [(i, (i + step * stride) % count) for i in range(count)]


def outgoing_rows(layer_out, frozen_out, control, row_kind, expert_ids, route_weights, experts_all, total_tokens):
    tok_rows, feat_cols = layer_out.shape
    capacity = tok_rows * 3 // 8
    flat_ids = expert_ids.reshape(-1)
    matches = (flat_ids[:, None] == jnp.arange(experts_all, dtype=jnp.int32)[None, :]).astype(jnp.int32)
    before = jnp.cumsum(matches, axis=0) - matches
    slot_idx = jnp.sum(before * matches, axis=1)
    column_idx = flat_ids * capacity + slot_idx
    columns = jnp.arange(experts_all * capacity, dtype=jnp.int32)
    placed = (
        (column_idx[:, None] == columns[None, :])
        .astype(jnp.float32)
        .reshape(tok_rows, 2, experts_all * capacity)
    )
    weighted = jnp.sum(placed * route_weights[:, :, None], axis=1)
    retain = (row_kind == 1)[:, None]
    target = jnp.where(retain, frozen_out.astype(jnp.float32), control[None, :])
    row_scale = jnp.where(retain, jnp.float32(retain_weight), jnp.float32(1.0))
    out_grad = row_scale * (layer_out.astype(jnp.float32) - target) * (1.0 / math.sqrt(total_tokens))
    rows = jnp.dot(weighted.T, out_grad, precision=lax.Precision.HIGHEST)
    return rows.reshape(experts_all, capacity, feat_cols).astype(jnp.bfloat16)


def product_kernel(place_ref, own_a, other_a, own_b0, own_b1, own_b2, own_b3, oth_b0, oth_b1, oth_b2, oth_b3,
                   g0, r1, l1, r2, l2, r3, l3, r4, l4, out_ref, rows_a, rows_b, *, tiles_a):
    step = pl.program_id(0)
    block, cols = g0.shape
    half = block // 2

    @pl.when(step == 0)
    def _():
        rep, dp = place_ref[0], place_ref[1]
        chip, core = rep // 2, lax.rem(rep, 2)

        def put(piece, offset, start, size):
            slot_block = lax.rem(dp + offset + 8, 8)
            from_chip, from_core = slot_block // 2, lax.rem(slot_block, 2)
            group = jnp.where(from_core == core, 0, 4)
            hop = jnp.where(from_core == 0, lax.rem(chip - from_chip + 4, 4), lax.rem(from_chip - chip + 4, 4))
            rows_a[pl.ds(pl.multiple_of((group + from_chip) * block + start, half), size), :] = piece[...]
            rows_b[pl.ds(pl.multiple_of((group + hop) * block + start, half), size), :] = piece[...]

        put(g0, 0, 0, block)
        put(r1, -1, 0, block)
        put(l1, 1, 0, block)
        put(r2, -2, 0, block)
        put(l2, 2, 0, block)
        put(r3, -3, 0, block)
        put(l3, 3, 0, block)
        put(r4, -4, 0, half)
        put(l4, 4, half, half)

    contract = (((0,), (0,)), ((), ()))

    @pl.when(step < tiles_a)
    def _():
        slots = jnp.concatenate([own_a[k] for k in range(4)] + [other_a[k] for k in range(4)], axis=0)
        out_ref[...] = lax.dot_general(slots, rows_a[...], contract, preferred_element_type=jnp.float32)

    @pl.when(step >= tiles_a)
    def _():
        slots = jnp.concatenate(
            [p[...] for p in (own_b0, own_b1, own_b2, own_b3, oth_b0, oth_b1, oth_b2, oth_b3)], axis=0
        )
        out_ref[...] = lax.dot_general(slots, rows_b[...], contract, preferred_element_type=jnp.float32)


def product(place, own_a, other_a, own_b, other_b, pieces):
    block, cols = pieces[0].shape
    tiles_a, tiles_b = own_a.shape[2] // tile, own_b[0].shape[1] // tile

    def at_a(i):
        return (0, 0, jnp.minimum(i, tiles_a - 1))

    def at_b(i):
        return (0, jnp.maximum(i - tiles_a, 0))

    in_specs = [pl.BlockSpec(memory_space=pltpu.SMEM)]
    in_specs += [pl.BlockSpec((4, block, tile), at_a)] * 2
    in_specs += [pl.BlockSpec((block, tile), at_b)] * 8
    in_specs += [
        pl.BlockSpec(p.shape, lambda i: (0, 0), pipeline_mode=pl.Buffered(1)) for p in pieces
    ]
    width = tile * (tiles_a + tiles_b)
    return pl.pallas_call(
        lambda *refs: product_kernel(*refs, tiles_a=tiles_a),
        grid=(tiles_a + tiles_b,),
        in_specs=in_specs,
        out_specs=pl.BlockSpec((tile, cols), lambda i: (i, 0)),
        out_shape=jax.ShapeDtypeStruct((width, cols), jnp.float32),
        scratch_shapes=[pltpu.VMEM((8 * block, cols), jnp.bfloat16)] * 2,
        compiler_params=pltpu.CompilerParams(vmem_limit_bytes=40 * 2**20),
        cost_estimate=pl.CostEstimate(
            flops=2 * 8 * block * cols * width, bytes_accessed=8 * block * (cols + width) * 2 + width * cols * 4, transcendentals=0
        ),
    )(place, own_a, other_a, *own_b, *other_b, *pieces)


def body(layer_out, frozen_out, control, row_kind, expert_ids, route_weights, hidden):
    exp_local, slots, width = hidden.shape
    dp_count = lax.axis_size("dp")
    exp_count = lax.axis_size("expert")
    total_tokens = layer_out.shape[0] * dp_count * exp_count
    held = hidden.reshape(slots, width)
    part_a, part_b = held[:, :split], held[:, split:]

    cores = [(i, i ^ 1) for i in range(8)]
    round_chips = [(2 * x + c, 2 * ((x + (1, -1)[c]) % 4) + c) for x in range(4) for c in range(2)]
    own_b = [part_b]
    for _ in range(3):
        own_b.append(lax.ppermute(own_b[-1], "rep", round_chips))
    other_b = [lax.ppermute(p, "rep", cores) for p in own_b]

    own_a = lax.all_to_all(
        jnp.broadcast_to(part_a[None], (4,) + part_a.shape), "rep", split_axis=0, concat_axis=0, tiled=True,
        axis_index_groups=[[0, 2, 4, 6], [1, 3, 5, 7]],
    )
    other_a = lax.ppermute(own_a, "rep", cores)

    grad_send = outgoing_rows(
        layer_out, frozen_out, control, row_kind, expert_ids, route_weights, exp_local * exp_count, total_tokens
    )
    mine = lax.all_to_all(grad_send, "expert", split_axis=0, concat_axis=0, tiled=True)
    mine = mine.reshape(-1, mine.shape[2])
    half = mine.shape[0] // 2
    pieces = [mine]
    right = left = mine
    for _ in range(3):
        right = lax.ppermute(right, "dp", ring(8, 1))
        left = lax.ppermute(left, "dp", ring(8, -1))
        pieces += [right, left]
    pieces.append(lax.ppermute(right[:half], "dp", ring(8, 1)))
    pieces.append(lax.ppermute(left[half:], "dp", ring(8, -1)))

    place = jnp.stack([lax.axis_index("rep"), lax.axis_index("dp")]).astype(jnp.int32)
    return product(place, own_a, other_a, own_b, other_b, pieces)[None]


def solution(mesh):
    in_specs = (
        P(("dp", "expert"), "rep"),
        P(("dp", "expert"), "rep"),
        P("rep"),
        P(("dp", "expert")),
        P(("dp", "expert"), None),
        P(("dp", "expert"), None),
        P("expert", "rep", "dp"),
    )
    out_specs = P("expert", "dp", "rep")
    return jax.shard_map(body, mesh=mesh, in_specs=in_specs, out_specs=out_specs, check_vma=False)
```

time: 129 us -> 142 us (1.10)
  blocking collectives: 91 us -> 0 us
  starting transfers between devices: 0.01 us -> 64.8 us
  waiting for transfers between devices: 0.71 us -> 41.5 us
  between operations: 13.4 us -> 0.37 us
  local copies, waits for them, and re-layouts: 7.09 us -> 19.2 us
  Pallas kernels: 0 us -> 11.4 us
  matrix products: 12.5 us -> 2.62 us
  other arithmetic: 3.57 us -> 0.95 us
    all_to_all x1 -> x0, blocking collectives: 91 us -> none  [spread(): lax.all_to_all(copies.astype(jnp.bfloat16), ('dp', 'expert'), split_axis=...]
    ppermute x0 -> x16, starting transfers between devices: none -> 51.7 us  [the longest x3 20.9 us: body(): left = lax.ppermute(left, 'dp', ring(8, -1))]
    all_to_all x0 -> x2, waiting for transfers between devices: none -> 28.1 us  [the longest x1 20.9 us: body(): lax.all_to_all(jnp.broadcast_to(part_a[None], (4,) + part_a.shape), 'rep'...]
    ppermute x0 -> x16, waiting for transfers between devices: none -> 13.4 us  [the longest x1 4.05 us: body(): pieces.append(lax.ppermute(right[:half], 'dp', ring(8, 1)))]
    all_to_all x0 -> x2, starting transfers between devices: none -> 13 us  [the longest x1 9.59 us: body(): lax.all_to_all(jnp.broadcast_to(part_a[None], (4,) + part_a.shape), 'rep'...]
    unnamed x1 -> x41, local copies, waits for them, and re-layouts: 0.79 us -> 13.2 us
    pallas_call x0 -> x1, Pallas kernels: none -> 11.4 us  [product(): pl.pallas_call(lambda *refs: product_kernel(*refs, tiles_a=tiles_a), grid...]
    dot_general x2 -> x1, matrix products: 12.5 us -> 2.62 us  [outgoing_rows(): rows = jnp.dot(weighted.T, out_grad, precision=lax.Precision.HIGHEST)]
  transfers between devices with their start and end apart: 1 -> 18, of which waited for: 0 -> 6; matrix products, arithmetic and copies ran while one was open for 6% -> 5% of each run, Pallas kernels for 0% -> 0%
where the time goes in v1:
time: 142 us; the launch traced here: 141 us
  starting transfers between devices  64.8 us (46%)
  waiting for transfers between devices  41.5 us (29%)
  local copies, waits for them, and re-layouts  19.2 us (14%)
  Pallas kernels  11.4 us (8%)
  matrix products  2.62 us (2%)
    ppermute x3, starting transfers between devices, body(): left = lax.ppermute(left, 'dp', ring(8, -1))  20.9 us
    all_to_all x1, waiting for transfers between devices, body(): lax.all_to_all(jnp.broadcast_to(part_a[None], (4,) + part_a.shape), 'rep'...  20.9 us
    unnamed x41, local copies, waits for them, and re-layouts  13.2 us
    pallas_call x1, Pallas kernels, product(): pl.pallas_call(lambda *refs: product_kernel(*refs, tiles_a=tiles_a), grid...  11.4 us
    all_to_all x1, starting transfers between devices, body(): lax.all_to_all(jnp.broadcast_to(part_a[None], (4,) + part_a.shape), 'rep'...  9.59 us
    ppermute x3, starting transfers between devices, body(): own_b.append(lax.ppermute(own_b[-1], 'rep', round_chips))  8.7 us
    ppermute x4, starting transfers between devices, body(): other_b = [lax.ppermute(p, 'rep', cores) for p in own_b]  8.63 us
    all_to_all x1, waiting for transfers between devices, body(): lax.all_to_all(grad_send, 'expert', split_axis=0, concat_axis=0, tiled=True)  7.28 us
  transfers between devices with their start and end apart: 18, of which 6 were waited for; matrix products, arithmetic and copies ran while one was open for 5% of the time, Pallas kernels for 0%

profile of v1, /device:TPU:6, one launch (start us, length us, event | category | flops | bytes accessed | tf_op | source)
XLA Modules:
  0.0 140.9 jit_solution(13377533047217910566)
XLA Ops:
  0.0 1.1 slice.24
  1.1 1.6 %broadcast_in_dim.39 = bf16[4,384,768]{2,1,0:T(8,128)(2,1)} broadcast(bf16[384,768]{1,0:T(8,128)(2,1)S(1)} %slice.24), dimensions={1,2} | broadcast | bytes 2949120 | tf_op jit(solution)/shard_map/broadcast_in_dim | solution.py:133
  2.7 9.6 %all-to-all-start = ((bf16[4,384,768]{2,1,0:T(8,128)(2,1)}), bf16[4,384,768]{2,1,0:T(8,128)(2,1)S(1)}, u32[]{:S(2)}, u32[]{:S(2)}) async-start(bf16[4,384,768]{2,1,0:T(8,128)(2,1)} %broadcast_in_dim.39), calls=%async_computation | async-start | bytes 4718592 | tf_op jit(solution)/shard_map/all_to_all | solution.py:132
  12.3 1.2 slice.25.refs_3_
  13.5 1.9 %collective-permute-start.1 = (bf16[384,1024]{1,0:T(8,128)(2,1)S(1)}, bf16[384,1024]{1,0:T(8,128)(2,1)}, u32[]{:S(2)}, u32[]{:S(2)}) collective-permute-start(bf16[384,1024]{1,0:T(8,128)(2,1)S(1)} %slice.25.refs_3_), channel_id=1, source_target_pairs={{0,128},{64,448},{128,256},{192,64},{256,384},{320,192},{384,0},{4... | collective-permute-start | bytes 2359304 | tf_op jit(solution)/shard_map/ppermute | solution.py:129
  15.4 0.1 copy.27
  15.5 0.1 eq.49
  15.7 0.1 eq.45
  15.8 0.6 reduce-window.6
  16.4 0.2 slice_reduce_fusion
  16.7 0.1 fusion.12
  16.8 0.1 reduce_sum.21
  16.9 0.1 copy.29
  17.0 0.1 select_reduce_fusion
  17.2 0.1 copy.30
  17.3 2.6 %convolution_convert_fusion = bf16[8,48,512]{2,1,0:T(8,128)(2,1)} fusion(f32[8,48,128]{2,1,0:T(8,128)S(1)} %bitcast.25, bf16[128,512]{1,0:T(8,128)(2,1)} %param.8, bf16[128,512]{1,0:T(8,128)(2,1)} %param.7, f32[512]{0:T(512)S(1)} %copy-done.17, f32[128]{0:T(128)S(1)} %broadcast_select_fusion, pred[128]{0:T(512)(128)(4,1)S(1)} %broadcast_compare_fusion), kind=kOutput, calls=%fused_computation | convolution fusion | flops 302579712 | bytes 854656 | tf_op jit(solution)/shard_map/dot_general | solution.py:38
  19.9 20.9 %all-to-all-done.refs_1_ = bf16[4,384,768]{2,1,0:T(8,128)(2,1)S(1)} async-done(((bf16[4,384,768]{2,1,0:T(8,128)(2,1)}), bf16[4,384,768]{2,1,0:T(8,128)(2,1)S(1)}, u32[]{:S(2)}, u32[]{:S(2)}) %all-to-all-start) | async-done | bytes 2359328 | tf_op jit(solution)/shard_map/all_to_all | solution.py:132
  40.8 3.5 %all-to-all-start.1 = ((bf16[8,48,512]{2,1,0:T(8,128)(2,1)}), bf16[8,48,512]{2,1,0:T(8,128)(2,1)S(1)}, u32[]{:S(2)}, u32[]{:S(2)}) async-start(bf16[8,48,512]{2,1,0:T(8,128)(2,1)} %convolution_convert_fusion), calls=%async_computation.1 | async-start | bytes 786432 | tf_op jit(solution)/shard_map/all_to_all | solution.py:141
  44.3 0.0 collective-permute-done.1.refs_4_
  44.3 2.6 %collective-permute-start.2 = (bf16[384,1024]{1,0:T(8,128)(2,1)}, bf16[384,1024]{1,0:T(8,128)(2,1)}, u32[]{:S(2)}, u32[]{:S(2)}) collective-permute-start(bf16[384,1024]{1,0:T(8,128)(2,1)} %collective-permute-done.1.refs_4_), channel_id=1, source_target_pairs={{0,128},{64,448},{128,256},{192,64},{256,384},{320,192},{384,0},{4... | collective-permute-start | bytes 2359304 | tf_op jit(solution)/shard_map/ppermute | solution.py:129
  46.9 1.9 %collective-permute-start = (bf16[4,384,768]{2,1,0:T(8,128)(2,1)S(1)}, bf16[4,384,768]{2,1,0:T(8,128)(2,1)}, u32[]{:S(2)}, u32[]{:S(2)}) collective-permute-start(bf16[4,384,768]{2,1,0:T(8,128)(2,1)S(1)} %all-to-all-done.refs_1_), channel_id=1, source_target_pairs={{0,64},{64,0},{128,192},{192,128},{256,320},{320,256},{384,448},{4... | collective-permute-start | bytes 7077896 | tf_op jit(solution)/shard_map/ppermute | solution.py:136
  48.8 7.3 %all-to-all-done.1 = bf16[8,48,512]{2,1,0:T(8,128)(2,1)S(1)} async-done(((bf16[8,48,512]{2,1,0:T(8,128)(2,1)}), bf16[8,48,512]{2,1,0:T(8,128)(2,1)S(1)}, u32[]{:S(2)}, u32[]{:S(2)}) %all-to-all-start.1) | async-done | bytes 393248 | tf_op jit(solution)/shard_map/all_to_all | solution.py:141
  56.1 10.2 %collective-permute-start.9 = (bf16[384,512]{1,0:T(8,128)(2,1)S(1)}, bf16[384,512]{1,0:T(8,128)(2,1)S(1)}, u32[]{:S(2)}, u32[]{:S(2)}) collective-permute-start(bf16[384,512]{1,0:T(8,128)(2,1)S(1)} %bitcast.19), channel_id=1, source_target_pairs={{0,56},{8,0},{16,8},{24,16},{32,24},{40,32},{48,40},{56,48},{1,57}... | collective-permute-start | bytes 1179656 | tf_op jit(solution)/shard_map/ppermute | solution.py:148
  66.3 1.9 %collective-permute-start.8 = (bf16[384,512]{1,0:T(8,128)(2,1)S(1)}, bf16[384,512]{1,0:T(8,128)(2,1)S(1)}, u32[]{:S(2)}, u32[]{:S(2)}) collective-permute-start(bf16[384,512]{1,0:T(8,128)(2,1)S(1)} %bitcast.20), channel_id=1, source_target_pairs={{0,8},{8,16},{16,24},{24,32},{32,40},{40,48},{48,56},{56,0},{1,9},... | collective-permute-start | bytes 1179656 | tf_op jit(solution)/shard_map/ppermute | solution.py:147
  68.2 3.3 %collective-permute-done.9.refs_13_ = bf16[384,512]{1,0:T(8,128)(2,1)S(1)} collective-permute-done((bf16[384,512]{1,0:T(8,128)(2,1)S(1)}, bf16[384,512]{1,0:T(8,128)(2,1)S(1)}, u32[]{:S(2)}, u32[]{:S(2)}) %collective-permute-start.9) | collective-permute-done | bytes 393248 | tf_op jit(solution)/shard_map/ppermute | solution.py:148
  71.6 5.6 %collective-permute-start.11 = (bf16[384,512]{1,0:T(8,128)(2,1)S(1)}, bf16[384,512]{1,0:T(8,128)(2,1)S(1)}, u32[]{:S(2)}, u32[]{:S(2)}) collective-permute-start(bf16[384,512]{1,0:T(8,128)(2,1)S(1)} %collective-permute-done.9.refs_13_), channel_id=1, source_target_pairs={{0,56},{8,0},{16,8},{24,16},{32,24},{40,32},{48,40},{56,48},{1,57}... | collective-permute-start | bytes 1179656 | tf_op jit(solution)/shard_map/ppermute | solution.py:148
  77.2 0.7 copy-done.8
  77.9 0.0 collective-permute-done.8.refs_12_
  77.9 1.9 %collective-permute-start.10 = (bf16[384,512]{1,0:T(8,128)(2,1)S(1)}, bf16[384,512]{1,0:T(8,128)(2,1)S(1)}, u32[]{:S(2)}, u32[]{:S(2)}) collective-permute-start(bf16[384,512]{1,0:T(8,128)(2,1)S(1)} %collective-permute-done.8.refs_12_), channel_id=1, source_target_pairs={{0,8},{8,16},{16,24},{24,32},{32,40},{40,48},{48,56},{56,0},{1,9},... | collective-permute-start | bytes 1179656 | tf_op jit(solution)/shard_map/ppermute | solution.py:147
  79.8 0.7 copy-done.10
  80.6 0.0 collective-permute-done.2.refs_5_
  80.6 4.2 %collective-permute-start.3 = (bf16[384,1024]{1,0:T(8,128)(2,1)}, bf16[384,1024]{1,0:T(8,128)(2,1)}, u32[]{:S(2)}, u32[]{:S(2)}) collective-permute-start(bf16[384,1024]{1,0:T(8,128)(2,1)} %collective-permute-done.2.refs_5_), channel_id=1, source_target_pairs={{0,128},{64,448},{128,256},{192,64},{256,384},{320,192},{384,0},{4... | collective-permute-start | bytes 2359304 | tf_op jit(solution)/shard_map/ppermute | solution.py:129
  84.7 0.0 collective-permute-done.11.refs_15_
  84.8 5.1 %collective-permute-start.13 = (bf16[384,512]{1,0:T(8,128)(2,1)S(1)}, bf16[384,512]{1,0:T(8,128)(2,1)S(1)}, u32[]{:S(2)}, u32[]{:S(2)}) collective-permute-start(bf16[384,512]{1,0:T(8,128)(2,1)S(1)} %collective-permute-done.11.refs_15_), channel_id=1, source_target_pairs={{0,56},{8,0},{16,8},{24,16},{32,24},{40,32},{48,40},{56,48},{1,57}... | collective-permute-start | bytes 1179656 | tf_op jit(solution)/shard_map/ppermute | solution.py:148
  89.9 0.8 copy-done.12
  90.7 1.9 %collective-permute-start.12 = (bf16[384,512]{1,0:T(8,128)(2,1)S(1)}, bf16[384,512]{1,0:T(8,128)(2,1)S(1)}, u32[]{:S(2)}, u32[]{:S(2)}) collective-permute-start(bf16[384,512]{1,0:T(8,128)(2,1)S(1)} %collective-permute-done.10.refs_14_), channel_id=1, source_target_pairs={{0,8},{8,16},{16,24},{24,32},{32,40},{40,48},{48,56},{56,0},{1,9},... | collective-permute-start | bytes 1179656 | tf_op jit(solution)/shard_map/ppermute | solution.py:147
  92.6 0.8 copy-done.14
  93.4 1.9 %collective-permute-start.4 = (bf16[384,1024]{1,0:T(8,128)(2,1)S(1)}, bf16[384,1024]{1,0:T(8,128)(2,1)S(1)}, u32[]{:S(2)}, u32[]{:S(2)}) collective-permute-start(bf16[384,1024]{1,0:T(8,128)(2,1)S(1)} %slice.25.refs_3_), channel_id=1, source_target_pairs={{0,64},{64,0},{128,192},{192,128},{256,320},{320,256},{384,448},{4... | collective-permute-start | bytes 2359304 | tf_op jit(solution)/shard_map/ppermute | solution.py:130
  95.3 2.4 %collective-permute-start.5 = (bf16[384,1024]{1,0:T(8,128)(2,1)}, bf16[384,1024]{1,0:T(8,128)(2,1)S(1)}, u32[]{:S(2)}, u32[]{:S(2)}) collective-permute-start(bf16[384,1024]{1,0:T(8,128)(2,1)} %collective-permute-done.1.refs_4_), channel_id=1, source_target_pairs={{0,64},{64,0},{128,192},{192,128},{256,320},{320,256},{384,448},{4... | collective-permute-start | bytes 2359304 | tf_op jit(solution)/shard_map/ppermute | solution.py:130
  97.7 3.8 %collective-permute-done.12.refs_16_ = bf16[384,512]{1,0:T(8,128)(2,1)S(1)} collective-permute-done((bf16[384,512]{1,0:T(8,128)(2,1)S(1)}, bf16[384,512]{1,0:T(8,128)(2,1)S(1)}, u32[]{:S(2)}, u32[]{:S(2)}) %collective-permute-start.12) | collective-permute-done | bytes 393248 | tf_op jit(solution)/shard_map/ppermute | solution.py:147
  101.5 1.9 %collective-permute-start.6 = (bf16[384,1024]{1,0:T(8,128)(2,1)}, bf16[384,1024]{1,0:T(8,128)(2,1)}, u32[]{:S(2)}, u32[]{:S(2)}) collective-permute-start(bf16[384,1024]{1,0:T(8,128)(2,1)} %collective-permute-done.2.refs_5_), channel_id=1, source_target_pairs={{0,64},{64,0},{128,192},{192,128},{256,320},{320,256},{384,448},{4... | collective-permute-start | bytes 2359304 | tf_op jit(solution)/shard_map/ppermute | solution.py:130
  103.5 0.0 collective-permute-done.3.refs_6_
  103.5 2.4 %collective-permute-start.7 = (bf16[384,1024]{1,0:T(8,128)(2,1)}, bf16[384,1024]{1,0:T(8,128)(2,1)}, u32[]{:S(2)}, u32[]{:S(2)}) collective-permute-start(bf16[384,1024]{1,0:T(8,128)(2,1)} %collective-permute-done.3.refs_6_), channel_id=1, source_target_pairs={{0,64},{64,0},{128,192},{192,128},{256,320},{320,256},{384,448},{4... | collective-permute-start | bytes 2359304 | tf_op jit(solution)/shard_map/ppermute | solution.py:130
  105.9 0.7 slice.28
  106.6 0.7 slice.27
  107.3 0.9 copy-done.4
  108.2 1.9 %collective-permute-start.15 = (bf16[192,512]{1,0:T(8,128)(2,1)}, bf16[192,512]{1,0:T(8,128)(2,1)}, u32[]{:S(2)}, u32[]{:S(2)}) collective-permute-start(bf16[192,512]{1,0:T(8,128)(2,1)} %slice.28), channel_id=1, source_target_pairs={{0,56},{8,0},{16,8},{24,16},{32,24},{40,32},{48,40},{56,48},{1,57}... | collective-permute-start | bytes 589832 | tf_op jit(solution)/shard_map/ppermute | solution.py:151
  110.1 0.0 collective-permute-done.5.refs_8_
  110.1 0.9 copy-done.6
  111.0 3.9 %collective-permute-start.14 = (bf16[192,512]{1,0:T(8,128)(2,1)}, bf16[192,512]{1,0:T(8,128)(2,1)}, u32[]{:S(2)}, u32[]{:S(2)}) collective-permute-start(bf16[192,512]{1,0:T(8,128)(2,1)} %slice.27), channel_id=1, source_target_pairs={{0,8},{8,16},{16,24},{24,32},{32,40},{40,48},{48,56},{56,0},{1,9},... | collective-permute-start | bytes 589832 | tf_op jit(solution)/shard_map/ppermute | solution.py:150
  114.9 0.1 pad_add_fusion.refs_0_
  115.0 2.2 %collective-permute-done.15.refs_19_ = bf16[192,512]{1,0:T(8,128)(2,1)} collective-permute-done((bf16[192,512]{1,0:T(8,128)(2,1)}, bf16[192,512]{1,0:T(8,128)(2,1)}, u32[]{:S(2)}, u32[]{:S(2)}) %collective-permute-start.15) | collective-permute-done | bytes 196640 | tf_op jit(solution)/shard_map/ppermute | solution.py:151
  117.2 4.0 %collective-permute-done.14.refs_18_ = bf16[192,512]{1,0:T(8,128)(2,1)} collective-permute-done((bf16[192,512]{1,0:T(8,128)(2,1)}, bf16[192,512]{1,0:T(8,128)(2,1)}, u32[]{:S(2)}, u32[]{:S(2)}) %collective-permute-start.14) | collective-permute-done | bytes 196640 | tf_op jit(solution)/shard_map/ppermute | solution.py:150
  121.2 0.0 collective-permute-done.6.refs_9_
  121.2 0.0 collective-permute-done.7.refs_10_
  121.3 1.0 copy-done.1
  122.2 1.0 copy-done.3
  123.2 1.1 copy-done.5
  124.4 1.1 copy-done.7
  125.5 1.0 copy-done.9
  126.5 1.0 copy-done.11
  127.5 1.0 copy-done.13
  128.5 1.0 copy-done.15
  129.5 11.4 %shard_map.73 = f32[1792,512]{1,0:T(8,128)} custom-call(s32[2]{0:T(128)S(1)} %pad_add_fusion.refs_0_, bf16[4,384,768]{2,1,0:T(8,128)(2,1)S(1)} %all-to-all-done.refs_1_, bf16[4,384,768]{2,1,0:T(8,128)(2,1)} %collective-permute-done.refs_2_, bf16[384,1024]{1,0:T(8,128)(2,1)S(1)} %slice.25.refs_3_, bf16[384,1024]{1,0:T(8,128)(2,1)} %collective-permute-done.1.refs_4_, ...), custom_call_target="tpu_custom_call" | custom-call | flops 5637144576 | bytes 17825792 | tf_op jit(solution)/shard_map/pallas_call | solution.py:103
  (36 shorter events, 0.1 us)
Async XLA Ops:
  2.7 12.8 %copy-start.16 = (s32[128,2]{0,1:T(2,128)S(1)}, s32[128,2]{0,1:T(2,128)}, u32[]{:S(2)}) copy-start(s32[128,2]{0,1:T(2,128)} %param.11) | copy-start | bytes 3076
  2.7 14.3 %copy-start.19 = (s32[128]{0:T(128)S(1)}, s32[128]{0:T(128)}, u32[]{:S(2)}) copy-start(s32[128]{0:T(128)} %param.10) | copy-start | bytes 1540
  2.7 14.4 %copy-start.18 = (f32[128,2]{0,1:T(2,128)S(1)}, f32[128,2]{0,1:T(2,128)}, u32[]{:S(2)}) copy-start(f32[128,2]{0,1:T(2,128)} %param.12) | copy-start | bytes 3076
  2.7 38.1 %all-to-all-start = ((bf16[4,384,768]{2,1,0:T(8,128)(2,1)}), bf16[4,384,768]{2,1,0:T(8,128)(2,1)S(1)}, u32[]{:S(2)}, u32[]{:S(2)}) async-start(bf16[4,384,768]{2,1,0:T(8,128)(2,1)} %broadcast_in_dim.39), calls=%async_computation | async-start | bytes 4718592 | tf_op jit(solution)/shard_map/all_to_all | solution.py:132
  12.3 5.1 %copy-start.17 = (f32[512]{0:T(512)S(1)}, f32[512]{0:T(512)}, u32[]{:S(2)}) copy-start(f32[512]{0:T(512)} %param.9) | copy-start | bytes 6148
  13.5 30.8 %collective-permute-start.1 = (bf16[384,1024]{1,0:T(8,128)(2,1)S(1)}, bf16[384,1024]{1,0:T(8,128)(2,1)}, u32[]{:S(2)}, u32[]{:S(2)}) collective-permute-start(bf16[384,1024]{1,0:T(8,128)(2,1)S(1)} %slice.25.refs_3_), channel_id=1, source_target_pairs={{0,128},{64,448},{128,256},{192,64},{256,384},{320,192},{384,0},{4... | collective-permute-start | bytes 2359304 | tf_op jit(solution)/shard_map/ppermute | solution.py:129
  40.8 15.3 %all-to-all-start.1 = ((bf16[8,48,512]{2,1,0:T(8,128)(2,1)}), bf16[8,48,512]{2,1,0:T(8,128)(2,1)S(1)}, u32[]{:S(2)}, u32[]{:S(2)}) async-start(bf16[8,48,512]{2,1,0:T(8,128)(2,1)} %convolution_convert_fusion), calls=%async_computation.1 | async-start | bytes 786432 | tf_op jit(solution)/shard_map/all_to_all | solution.py:141
  44.3 36.3 %collective-permute-start.2 = (bf16[384,1024]{1,0:T(8,128)(2,1)}, bf16[384,1024]{1,0:T(8,128)(2,1)}, u32[]{:S(2)}, u32[]{:S(2)}) collective-permute-start(bf16[384,1024]{1,0:T(8,128)(2,1)} %collective-permute-done.1.refs_4_), channel_id=1, source_target_pairs={{0,128},{64,448},{128,256},{192,64},{256,384},{320,192},{384,0},{4... | collective-permute-start | bytes 2359304 | tf_op jit(solution)/shard_map/ppermute | solution.py:129
  46.9 74.4 %collective-permute-start = (bf16[4,384,768]{2,1,0:T(8,128)(2,1)S(1)}, bf16[4,384,768]{2,1,0:T(8,128)(2,1)}, u32[]{:S(2)}, u32[]{:S(2)}) collective-permute-start(bf16[4,384,768]{2,1,0:T(8,128)(2,1)S(1)} %all-to-all-done.refs_1_), channel_id=1, source_target_pairs={{0,64},{64,0},{128,192},{192,128},{256,320},{320,256},{384,448},{4... | collective-permute-start | bytes 7077896 | tf_op jit(solution)/shard_map/ppermute | solution.py:136
  56.1 15.5 %collective-permute-start.9 = (bf16[384,512]{1,0:T(8,128)(2,1)S(1)}, bf16[384,512]{1,0:T(8,128)(2,1)S(1)}, u32[]{:S(2)}, u32[]{:S(2)}) collective-permute-start(bf16[384,512]{1,0:T(8,128)(2,1)S(1)} %bitcast.19), channel_id=1, source_target_pairs={{0,56},{8,0},{16,8},{24,16},{32,24},{40,32},{48,40},{56,48},{1,57}... | collective-permute-start | bytes 1179656 | tf_op jit(solution)/shard_map/ppermute | solution.py:148
  66.3 11.6 %collective-permute-start.8 = (bf16[384,512]{1,0:T(8,128)(2,1)S(1)}, bf16[384,512]{1,0:T(8,128)(2,1)S(1)}, u32[]{:S(2)}, u32[]{:S(2)}) collective-permute-start(bf16[384,512]{1,0:T(8,128)(2,1)S(1)} %bitcast.20), channel_id=1, source_target_pairs={{0,8},{8,16},{16,24},{24,32},{32,40},{40,48},{48,56},{56,0},{1,9},... | collective-permute-start | bytes 1179656 | tf_op jit(solution)/shard_map/ppermute | solution.py:147
  71.6 13.2 %collective-permute-start.11 = (bf16[384,512]{1,0:T(8,128)(2,1)S(1)}, bf16[384,512]{1,0:T(8,128)(2,1)S(1)}, u32[]{:S(2)}, u32[]{:S(2)}) collective-permute-start(bf16[384,512]{1,0:T(8,128)(2,1)S(1)} %collective-permute-done.9.refs_13_), channel_id=1, source_target_pairs={{0,56},{8,0},{16,8},{24,16},{32,24},{40,32},{48,40},{56,48},{1,57}... | collective-permute-start | bytes 1179656 | tf_op jit(solution)/shard_map/ppermute | solution.py:148
  77.2 0.7 copy-start.8
  77.9 12.8 %collective-permute-start.10 = (bf16[384,512]{1,0:T(8,128)(2,1)S(1)}, bf16[384,512]{1,0:T(8,128)(2,1)S(1)}, u32[]{:S(2)}, u32[]{:S(2)}) collective-permute-start(bf16[384,512]{1,0:T(8,128)(2,1)S(1)} %collective-permute-done.8.refs_12_), channel_id=1, source_target_pairs={{0,8},{8,16},{16,24},{24,32},{32,40},{40,48},{48,56},{56,0},{1,9},... | collective-permute-start | bytes 1179656 | tf_op jit(solution)/shard_map/ppermute | solution.py:147
  79.8 0.7 copy-start.10
  80.6 22.9 %collective-permute-start.3 = (bf16[384,1024]{1,0:T(8,128)(2,1)}, bf16[384,1024]{1,0:T(8,128)(2,1)}, u32[]{:S(2)}, u32[]{:S(2)}) collective-permute-start(bf16[384,1024]{1,0:T(8,128)(2,1)} %collective-permute-done.2.refs_5_), channel_id=1, source_target_pairs={{0,128},{64,448},{128,256},{192,64},{256,384},{320,192},{384,0},{4... | collective-permute-start | bytes 2359304 | tf_op jit(solution)/shard_map/ppermute | solution.py:129
  84.8 10.6 %collective-permute-start.13 = (bf16[384,512]{1,0:T(8,128)(2,1)S(1)}, bf16[384,512]{1,0:T(8,128)(2,1)S(1)}, u32[]{:S(2)}, u32[]{:S(2)}) collective-permute-start(bf16[384,512]{1,0:T(8,128)(2,1)S(1)} %collective-permute-done.11.refs_15_), channel_id=1, source_target_pairs={{0,56},{8,0},{16,8},{24,16},{32,24},{40,32},{48,40},{56,48},{1,57}... | collective-permute-start | bytes 1179656 | tf_op jit(solution)/shard_map/ppermute | solution.py:148
  89.9 0.8 copy-start.12
  90.7 10.9 %collective-permute-start.12 = (bf16[384,512]{1,0:T(8,128)(2,1)S(1)}, bf16[384,512]{1,0:T(8,128)(2,1)S(1)}, u32[]{:S(2)}, u32[]{:S(2)}) collective-permute-start(bf16[384,512]{1,0:T(8,128)(2,1)S(1)} %collective-permute-done.10.refs_14_), channel_id=1, source_target_pairs={{0,8},{8,16},{16,24},{24,32},{32,40},{40,48},{48,56},{56,0},{1,9},... | collective-permute-start | bytes 1179656 | tf_op jit(solution)/shard_map/ppermute | solution.py:147
  92.6 0.8 copy-start.14
  93.4 13.9 %collective-permute-start.4 = (bf16[384,1024]{1,0:T(8,128)(2,1)S(1)}, bf16[384,1024]{1,0:T(8,128)(2,1)S(1)}, u32[]{:S(2)}, u32[]{:S(2)}) collective-permute-start(bf16[384,1024]{1,0:T(8,128)(2,1)S(1)} %slice.25.refs_3_), channel_id=1, source_target_pairs={{0,64},{64,0},{128,192},{192,128},{256,320},{320,256},{384,448},{4... | collective-permute-start | bytes 2359304 | tf_op jit(solution)/shard_map/ppermute | solution.py:130
  95.3 12.0 %copy-start = (bf16[384,512]{1,0:T(8,128)(2,1)}, bf16[384,512]{1,0:T(8,128)(2,1)S(1)}, u32[]{:S(2)}) copy-start(bf16[384,512]{1,0:T(8,128)(2,1)S(1)} %collective-permute-done.13.refs_17_) | copy-start | bytes 1179652
  95.3 14.8 %collective-permute-start.5 = (bf16[384,1024]{1,0:T(8,128)(2,1)}, bf16[384,1024]{1,0:T(8,128)(2,1)S(1)}, u32[]{:S(2)}, u32[]{:S(2)}) collective-permute-start(bf16[384,1024]{1,0:T(8,128)(2,1)} %collective-permute-done.1.refs_4_), channel_id=1, source_target_pairs={{0,64},{64,0},{128,192},{192,128},{256,320},{320,256},{384,448},{4... | collective-permute-start | bytes 2359304 | tf_op jit(solution)/shard_map/ppermute | solution.py:130
  101.5 8.5 %copy-start.2 = (bf16[384,512]{1,0:T(8,128)(2,1)}, bf16[384,512]{1,0:T(8,128)(2,1)S(1)}, u32[]{:S(2)}) copy-start(bf16[384,512]{1,0:T(8,128)(2,1)S(1)} %collective-permute-done.12.refs_16_) | copy-start | bytes 1179652
  101.5 19.7 %collective-permute-start.6 = (bf16[384,1024]{1,0:T(8,128)(2,1)}, bf16[384,1024]{1,0:T(8,128)(2,1)}, u32[]{:S(2)}, u32[]{:S(2)}) collective-permute-start(bf16[384,1024]{1,0:T(8,128)(2,1)} %collective-permute-done.2.refs_5_), channel_id=1, source_target_pairs={{0,64},{64,0},{128,192},{192,128},{256,320},{320,256},{384,448},{4... | collective-permute-start | bytes 2359304 | tf_op jit(solution)/shard_map/ppermute | solution.py:130
  103.5 17.8 %collective-permute-start.7 = (bf16[384,1024]{1,0:T(8,128)(2,1)}, bf16[384,1024]{1,0:T(8,128)(2,1)}, u32[]{:S(2)}, u32[]{:S(2)}) collective-permute-start(bf16[384,1024]{1,0:T(8,128)(2,1)} %collective-permute-done.3.refs_6_), channel_id=1, source_target_pairs={{0,64},{64,0},{128,192},{192,128},{256,320},{320,256},{384,448},{4... | collective-permute-start | bytes 2359304 | tf_op jit(solution)/shard_map/ppermute | solution.py:130
  107.3 0.9 copy-start.4
  108.2 9.0 %collective-permute-start.15 = (bf16[192,512]{1,0:T(8,128)(2,1)}, bf16[192,512]{1,0:T(8,128)(2,1)}, u32[]{:S(2)}, u32[]{:S(2)}) collective-permute-start(bf16[192,512]{1,0:T(8,128)(2,1)} %slice.28), channel_id=1, source_target_pairs={{0,56},{8,0},{16,8},{24,16},{32,24},{40,32},{48,40},{56,48},{1,57}... | collective-permute-start | bytes 589832 | tf_op jit(solution)/shard_map/ppermute | solution.py:151
  110.1 0.9 copy-start.6
  111.0 10.2 %collective-permute-start.14 = (bf16[192,512]{1,0:T(8,128)(2,1)}, bf16[192,512]{1,0:T(8,128)(2,1)}, u32[]{:S(2)}, u32[]{:S(2)}) collective-permute-start(bf16[192,512]{1,0:T(8,128)(2,1)} %slice.27), channel_id=1, source_target_pairs={{0,8},{8,16},{16,24},{24,32},{32,40},{40,48},{48,56},{56,0},{1,9},... | collective-permute-start | bytes 589832 | tf_op jit(solution)/shard_map/ppermute | solution.py:150
  121.2 1.0 copy-start.1
  122.2 1.0 copy-start.3
  123.2 1.1 copy-start.5
  124.4 1.1 copy-start.7
  125.5 1.0 copy-start.9
  126.5 1.0 copy-start.11
  127.5 1.0 copy-start.13
  128.5 1.0 copy-start.15

commit v2 on v0

v2 whole, which is shorter than its diff:
```python
import math

import jax
import jax.numpy as jnp
from jax import lax
from jax.experimental import pallas as pl
from jax.experimental.pallas import tpu as pltpu
from jax.sharding import PartitionSpec as P

retain_weight = 2.0
tile = 256


def rows_kernel(lo_ref, fr_ref, control_ref, kind_ref, ids_ref, weights_ref, out_ref, *, experts, scale):
    tokens, feats = lo_ref.shape
    capacity = out_ref.shape[0] // experts
    down = lax.broadcasted_iota(jnp.int32, (tokens, tokens), 0)
    across = lax.broadcasted_iota(jnp.int32, (tokens, tokens), 1)
    earlier = (down < across).astype(jnp.float32)
    expert = lax.broadcasted_iota(jnp.int32, (experts, tokens), 0)
    first, second = ids_ref[0:1, :] == expert, ids_ref[1:2, :] == expert
    named = (first | second).astype(jnp.float32)
    weight = jnp.where(first, weights_ref[0:1, :], 0.0) + jnp.where(second, weights_ref[1:2, :], 0.0)
    slot = jnp.dot(named, earlier, preferred_element_type=jnp.float32).astype(jnp.int32)
    slot = jnp.where(first | second, slot, -1)
    wanted = lax.broadcasted_iota(jnp.int32, (experts, capacity, tokens), 1)
    placed = jnp.where(slot[:, None, :] == wanted, weight[:, None, :], 0.0)
    placed = placed.reshape(experts * capacity, tokens)
    kind = jnp.sum(jnp.where(down == across, kind_ref[...], 0), axis=1, keepdims=True)
    retain = kind == 1
    target = jnp.where(retain, fr_ref[...].astype(jnp.float32), control_ref[...])
    factor = jnp.where(retain, jnp.float32(retain_weight), jnp.float32(1.0))
    out_grad = factor * (lo_ref[...].astype(jnp.float32) - target) * scale
    rows = jnp.dot(placed, out_grad, precision=lax.Precision.HIGHEST, preferred_element_type=jnp.float32)
    out_ref[...] = rows.astype(jnp.bfloat16)


def outgoing_rows(layer_out, frozen_out, control, row_kind, expert_ids, route_weights, experts_all, total_tokens):
    tokens, feats = layer_out.shape
    capacity = tokens * 3 // 8
    rows = pl.pallas_call(
        lambda *refs: rows_kernel(*refs, experts=experts_all, scale=1.0 / math.sqrt(total_tokens)),
        out_shape=jax.ShapeDtypeStruct((experts_all * capacity, feats), jnp.bfloat16),
        compiler_params=pltpu.CompilerParams(vmem_limit_bytes=60 * 2**20),
    )(layer_out, frozen_out, control[None, :], row_kind[None, :], expert_ids.T, route_weights.T)
    return rows.reshape(experts_all, capacity, feats)


def product_kernel(place_ref, slots, *refs):
    pieces, (out_ref, rows) = refs[:-2], refs[-2:]
    block = pieces[0].shape[0]

    @pl.when(pl.program_id(0) == 0)
    def _():
        rep, dp = place_ref[0], place_ref[1]
        way = jnp.where(lax.rem(rep, 2) == 0, -1, 1)
        for piece, hops in zip(pieces, (0, 1, 2, 3, 4, -1, -2, -3)):
            slot_block = lax.rem(dp + way * hops + 8, 8)
            rows[pl.ds(pl.multiple_of(slot_block * block, block), block), :] = piece[...]

    out_ref[...] = lax.dot_general(
        slots[...], rows[...], (((0,), (0,)), ((), ())), preferred_element_type=jnp.float32
    )


def product(place, slots, pieces):
    block, cols = pieces[0].shape
    width = slots.shape[1]
    in_specs = [pl.BlockSpec(memory_space=pltpu.SMEM)]
    in_specs += [pl.BlockSpec((8 * block, tile), lambda i: (0, i))]
    in_specs += [pl.BlockSpec(p.shape, lambda i: (0, 0), pipeline_mode=pl.Buffered(1)) for p in pieces]
    return pl.pallas_call(
        product_kernel,
        grid=(width // tile,),
        in_specs=in_specs,
        out_specs=pl.BlockSpec((tile, cols), lambda i: (i, 0)),
        out_shape=jax.ShapeDtypeStruct((width, cols), jnp.float32),
        scratch_shapes=[pltpu.VMEM((8 * block, cols), jnp.bfloat16)],
        compiler_params=pltpu.CompilerParams(vmem_limit_bytes=52 * 2**20),
        cost_estimate=pl.CostEstimate(
            flops=2 * 8 * block * cols * width, bytes_accessed=8 * block * (cols + width) * 2 + width * cols * 4, transcendentals=0
        ),
    )(place, slots, *pieces)


def body(layer_out, frozen_out, control, row_kind, expert_ids, route_weights, hidden):
    exp_local, slots, width = hidden.shape
    dp_count = lax.axis_size("dp")
    exp_count = lax.axis_size("expert")
    total_tokens = layer_out.shape[0] * dp_count * exp_count

    grad_send = outgoing_rows(
        layer_out, frozen_out, control, row_kind, expert_ids, route_weights, exp_local * exp_count, total_tokens
    )
    every_slot = lax.all_gather(hidden.reshape(slots, width), "rep", axis=0, tiled=True)
    mine = lax.all_to_all(grad_send, "expert", split_axis=0, concat_axis=0, tiled=True)
    mine = mine.reshape(-1, mine.shape[2])
    cores = [(i, i ^ 1) for i in range(8)]
    round_dp = [(r * 8 + d, r * 8 + (d + (1, -1)[r % 2]) % 8) for r in range(8) for d in range(8)]

    def next_dp(part):
        return lax.ppermute(part, ("rep", "dp"), round_dp)

    def other_core(part):
        return lax.ppermute(part, "rep", cores)

    ours1, pair0 = next_dp(mine), other_core(mine)
    pair1, ours2 = next_dp(pair0), next_dp(ours1)
    back1, pair2, ours3 = other_core(pair1), next_dp(pair1), next_dp(ours2)
    back2, pair3, ours4 = other_core(pair2), next_dp(pair2), next_dp(ours3)
    back3 = other_core(pair3)
    pieces = [mine, ours1, ours2, ours3, ours4, back1, back2, back3]

    place = jnp.stack([lax.axis_index("rep"), lax.axis_index("dp")]).astype(jnp.int32)
    return product(place, every_slot, pieces)[None]


def solution(mesh):
    in_specs = (
        P(("dp", "expert"), "rep"),
        P(("dp", "expert"), "rep"),
        P("rep"),
        P(("dp", "expert")),
        P(("dp", "expert"), None),
        P(("dp", "expert"), None),
        P("expert", "rep", "dp"),
    )
    out_specs = P("expert", "dp", "rep")
    return jax.shard_map(body, mesh=mesh, in_specs=in_specs, out_specs=out_specs, check_vma=False)
```

time: 129 us -> 103 us (0.80)
  blocking collectives: 91 us -> 21.8 us
  starting transfers between devices: 0.01 us -> 27.9 us
  waiting for transfers between devices: 0.71 us -> 24.9 us
  Pallas kernels: 0 us -> 14.4 us
  matrix products: 12.5 us -> 0 us
  local copies, waits for them, and re-layouts: 7.09 us -> 0.01 us
  other arithmetic: 3.57 us -> 0.08 us
    all_to_all x1, blocking collectives: 91 us -> 21.8 us  [body(): lax.all_to_all(grad_send, 'expert', split_axis=0, concat_axis=0, tiled=True)]
    ppermute x0 -> x11, starting transfers between devices: none -> 27.9 us  [the longest x7 18.1 us: next_dp(): return lax.ppermute(part, ('rep', 'dp'), round_dp)]
    ppermute x0 -> x11, waiting for transfers between devices: none -> 24.2 us  [the longest x7 24.2 us: next_dp(): return lax.ppermute(part, ('rep', 'dp'), round_dp)]
    pallas_call x0 -> x2, Pallas kernels: none -> 14.4 us  [the longest x1 11.7 us: product(): pl.pallas_call(product_kernel, grid=(width // tile,), in_specs=in_specs,...]
    dot_general x2 -> x0, matrix products: 12.5 us -> none  [the longest x1 10.6 us: body(): jnp.einsum('jmf,jmd->jfd', lax.all_gather(hidden, 'rep', axis=1, tiled=Tr...]
    dot_general x2 -> x0, local copies, waits for them, and re-layouts: 5.23 us -> none  [the longest x1 5.11 us: body(): jnp.einsum('jmf,jmd->jfd', lax.all_gather(hidden, 'rep', axis=1, tiled=Tr...]
  transfers between devices with their start and end apart: 1 -> 12, of which waited for: 0 -> 6; matrix products, arithmetic and copies ran while one was open for 6% -> 0% of each run, Pallas kernels for 0% -> 3%
where the time goes in v2:
time: 103 us
  starting transfers between devices  27.9 us (27%)
  waiting for transfers between devices  24.9 us (24%)
  blocking collectives  21.8 us (21%)
  Pallas kernels  14.4 us (14%)
  between operations  13.5 us (13%)
    ppermute x7, waiting for transfers between devices, next_dp(): return lax.ppermute(part, ('rep', 'dp'), round_dp)  24.2 us
    all_to_all x1, blocking collectives, body(): lax.all_to_all(grad_send, 'expert', split_axis=0, concat_axis=0, tiled=True)  21.8 us
    ppermute x7, starting transfers between devices, next_dp(): return lax.ppermute(part, ('rep', 'dp'), round_dp)  18.1 us
    pallas_call x1, Pallas kernels, product(): pl.pallas_call(product_kernel, grid=(width // tile,), in_specs=in_specs,...  11.7 us
    ppermute x4, starting transfers between devices, other_core(): return lax.ppermute(part, 'rep', cores)  9.76 us
    pallas_call x1, Pallas kernels, outgoing_rows(): pl.pallas_call(lambda *refs: rows_kernel(*refs, experts=experts_all, scal...  2.68 us
  transfers between devices with their start and end apart: 12, of which 6 were waited for; matrix products, arithmetic and copies ran while one was open for 0% of the time, Pallas kernels for 3%

profile of v2, /device:TPU:6, one launch (start us, length us, event | category | flops | bytes accessed | tf_op | source)
XLA Modules:
  0.0 102.6 jit_solution(17199816017554854429)
XLA Ops:
  6.5 0.0 all-gather.3.cloned.1.call-start
  6.5 0.7 all-gather.3.cloned.1.call-update
  7.3 2.7 %shard_map.73 = bf16[384,512]{1,0:T(8,128)(2,1)} custom-call(bf16[128,512]{1,0:T(8,128)(2,1)} %refs_0_.1, bf16[128,512]{1,0:T(8,128)(2,1)} %refs_1_.1, f32[1,512]{1,0:T(1,128)} %bitcast.14, s32[1,128]{1,0:T(1,128)} %bitcast.17, s32[2,128]{1,0:T(2,128)} %bitcast.15, f32[2,128]{1,0:T(2,128)} %bitcast.16), custom_call_target="tpu_custom_call" | custom-call | tf_op jit(solution)/shard_map/pallas_call | solution.py:41
  9.9 21.8 %all_to_all.5 = bf16[8,48,512]{2,1,0:T(8,128)(2,1)S(1)} all-to-all(bf16[8,48,512]{2,1,0:T(8,128)(2,1)} %bitcast.13), channel_id=1, replica_groups=mesh['rep'=8,'dp'=8,'expert'=8] {'expert'}, dimensions={0} | all-to-all | bytes 786432 | tf_op jit(solution)/shard_map/all_to_all | solution.py:96
  31.7 1.9 %collective-permute-start.4 = (bf16[384,512]{1,0:T(8,128)(2,1)S(1)}, bf16[384,512]{1,0:T(8,128)(2,1)S(1)}, u32[]{:S(2)}, u32[]{:S(2)}) collective-permute-start(bf16[384,512]{1,0:T(8,128)(2,1)S(1)} %bitcast.10), channel_id=1, source_target_pairs={{0,64},{64,0},{128,192},{192,128},{256,320},{320,256},{384,448},{4... | collective-permute-start | bytes 1179656 | tf_op jit(solution)/shard_map/ppermute | solution.py:105
  33.6 4.3 %collective-permute-start = (bf16[384,512]{1,0:T(8,128)(2,1)S(1)}, bf16[384,512]{1,0:T(8,128)(2,1)S(1)}, u32[]{:S(2)}, u32[]{:S(2)}) collective-permute-start(bf16[384,512]{1,0:T(8,128)(2,1)S(1)} %bitcast.11), channel_id=1, source_target_pairs={{0,8},{8,16},{16,24},{24,32},{32,40},{40,48},{48,56},{56,0},{64,12... | collective-permute-start | bytes 1179656 | tf_op jit(solution)/shard_map/ppermute | solution.py:102
  37.9 0.0 collective-permute-done.4
  37.9 4.3 %collective-permute-start.5 = (bf16[384,512]{1,0:T(8,128)(2,1)S(1)}, bf16[384,512]{1,0:T(8,128)(2,1)S(1)}, u32[]{:S(2)}, u32[]{:S(2)}) collective-permute-start(bf16[384,512]{1,0:T(8,128)(2,1)S(1)} %collective-permute-done.4), channel_id=1, source_target_pairs={{0,8},{8,16},{16,24},{24,32},{32,40},{40,48},{48,56},{56,0},{64,12... | collective-permute-start | bytes 1179656 | tf_op jit(solution)/shard_map/ppermute | solution.py:102
  42.2 8.1 %collective-permute-done.refs_1_ = bf16[384,512]{1,0:T(8,128)(2,1)S(1)} collective-permute-done((bf16[384,512]{1,0:T(8,128)(2,1)S(1)}, bf16[384,512]{1,0:T(8,128)(2,1)S(1)}, u32[]{:S(2)}, u32[]{:S(2)}) %collective-permute-start) | collective-permute-done | bytes 393248 | tf_op jit(solution)/shard_map/ppermute | solution.py:102
  50.3 1.9 %collective-permute-start.1 = (bf16[384,512]{1,0:T(8,128)(2,1)S(1)}, bf16[384,512]{1,0:T(8,128)(2,1)S(1)}, u32[]{:S(2)}, u32[]{:S(2)}) collective-permute-start(bf16[384,512]{1,0:T(8,128)(2,1)S(1)} %collective-permute-done.refs_1_), channel_id=1, source_target_pairs={{0,8},{8,16},{16,24},{24,32},{32,40},{40,48},{48,56},{56,0},{64,12... | collective-permute-start | bytes 1179656 | tf_op jit(solution)/shard_map/ppermute | solution.py:102
  52.3 2.3 %collective-permute-done.5 = bf16[384,512]{1,0:T(8,128)(2,1)S(1)} collective-permute-done((bf16[384,512]{1,0:T(8,128)(2,1)S(1)}, bf16[384,512]{1,0:T(8,128)(2,1)S(1)}, u32[]{:S(2)}, u32[]{:S(2)}) %collective-permute-start.5) | collective-permute-done | bytes 393248 | tf_op jit(solution)/shard_map/ppermute | solution.py:102
  54.6 1.9 %collective-permute-start.7 = (bf16[384,512]{1,0:T(8,128)(2,1)S(1)}, bf16[384,512]{1,0:T(8,128)(2,1)S(1)}, u32[]{:S(2)}, u32[]{:S(2)}) collective-permute-start(bf16[384,512]{1,0:T(8,128)(2,1)S(1)} %collective-permute-done.5), channel_id=1, source_target_pairs={{0,8},{8,16},{16,24},{24,32},{32,40},{40,48},{48,56},{56,0},{64,12... | collective-permute-start | bytes 1179656 | tf_op jit(solution)/shard_map/ppermute | solution.py:102
  56.5 4.7 %collective-permute-done.1.refs_2_ = bf16[384,512]{1,0:T(8,128)(2,1)S(1)} collective-permute-done((bf16[384,512]{1,0:T(8,128)(2,1)S(1)}, bf16[384,512]{1,0:T(8,128)(2,1)S(1)}, u32[]{:S(2)}, u32[]{:S(2)}) %collective-permute-start.1) | collective-permute-done | bytes 393248 | tf_op jit(solution)/shard_map/ppermute | solution.py:102
  61.2 1.9 %collective-permute-start.2 = (bf16[384,512]{1,0:T(8,128)(2,1)S(1)}, bf16[384,512]{1,0:T(8,128)(2,1)S(1)}, u32[]{:S(2)}, u32[]{:S(2)}) collective-permute-start(bf16[384,512]{1,0:T(8,128)(2,1)S(1)} %collective-permute-done.1.refs_2_), channel_id=1, source_target_pairs={{0,8},{8,16},{16,24},{24,32},{32,40},{40,48},{48,56},{56,0},{64,12... | collective-permute-start | bytes 1179656 | tf_op jit(solution)/shard_map/ppermute | solution.py:102
  63.1 2.3 %collective-permute-done.7 = bf16[384,512]{1,0:T(8,128)(2,1)S(1)} collective-permute-done((bf16[384,512]{1,0:T(8,128)(2,1)S(1)}, bf16[384,512]{1,0:T(8,128)(2,1)S(1)}, u32[]{:S(2)}, u32[]{:S(2)}) %collective-permute-start.7) | collective-permute-done | bytes 393248 | tf_op jit(solution)/shard_map/ppermute | solution.py:102
  65.4 1.9 %collective-permute-start.9 = (bf16[384,512]{1,0:T(8,128)(2,1)S(1)}, bf16[384,512]{1,0:T(8,128)(2,1)}, u32[]{:S(2)}, u32[]{:S(2)}) collective-permute-start(bf16[384,512]{1,0:T(8,128)(2,1)S(1)} %collective-permute-done.7), channel_id=1, source_target_pairs={{0,8},{8,16},{16,24},{24,32},{32,40},{40,48},{48,56},{56,0},{64,12... | collective-permute-start | bytes 1179656 | tf_op jit(solution)/shard_map/ppermute | solution.py:102
  67.3 3.8 %collective-permute-start.6 = (bf16[384,512]{1,0:T(8,128)(2,1)S(1)}, bf16[384,512]{1,0:T(8,128)(2,1)S(1)}, u32[]{:S(2)}, u32[]{:S(2)}) collective-permute-start(bf16[384,512]{1,0:T(8,128)(2,1)S(1)} %collective-permute-done.5), channel_id=1, source_target_pairs={{0,64},{64,0},{128,192},{192,128},{256,320},{320,256},{384,448},{4... | collective-permute-start | bytes 1179656 | tf_op jit(solution)/shard_map/ppermute | solution.py:105
  71.2 1.9 %collective-permute-start.8 = (bf16[384,512]{1,0:T(8,128)(2,1)S(1)}, bf16[384,512]{1,0:T(8,128)(2,1)S(1)}, u32[]{:S(2)}, u32[]{:S(2)}) collective-permute-start(bf16[384,512]{1,0:T(8,128)(2,1)S(1)} %collective-permute-done.7), channel_id=1, source_target_pairs={{0,64},{64,0},{128,192},{192,128},{256,320},{320,256},{384,448},{4... | collective-permute-start | bytes 1179656 | tf_op jit(solution)/shard_map/ppermute | solution.py:105
  73.1 0.0 collective-permute-done.2.refs_3_
  73.1 1.9 %collective-permute-start.3 = (bf16[384,512]{1,0:T(8,128)(2,1)S(1)}, bf16[384,512]{1,0:T(8,128)(2,1)S(1)}, u32[]{:S(2)}, u32[]{:S(2)}) collective-permute-start(bf16[384,512]{1,0:T(8,128)(2,1)S(1)} %collective-permute-done.2.refs_3_), channel_id=1, source_target_pairs={{0,8},{8,16},{16,24},{24,32},{32,40},{40,48},{48,56},{56,0},{64,12... | collective-permute-start | bytes 1179656 | tf_op jit(solution)/shard_map/ppermute | solution.py:102
  75.1 1.3 %collective-permute-done.9 = bf16[384,512]{1,0:T(8,128)(2,1)} collective-permute-done((bf16[384,512]{1,0:T(8,128)(2,1)S(1)}, bf16[384,512]{1,0:T(8,128)(2,1)}, u32[]{:S(2)}, u32[]{:S(2)}) %collective-permute-start.9) | collective-permute-done | bytes 393248 | tf_op jit(solution)/shard_map/ppermute | solution.py:102
  76.4 2.1 %collective-permute-start.10 = (bf16[384,512]{1,0:T(8,128)(2,1)}, bf16[384,512]{1,0:T(8,128)(2,1)}, u32[]{:S(2)}, u32[]{:S(2)}) collective-permute-start(bf16[384,512]{1,0:T(8,128)(2,1)} %collective-permute-done.9), channel_id=1, source_target_pairs={{0,64},{64,0},{128,192},{192,128},{256,320},{320,256},{384,448},{4... | collective-permute-start | bytes 1179656 | tf_op jit(solution)/shard_map/ppermute | solution.py:105
  78.5 0.1 pad_add_fusion.place_ref
  78.6 0.0 collective-permute-done.6.refs_5_
  78.6 0.0 copy-start
  78.6 0.0 collective-permute-done.8.refs_6_
  78.6 0.0 copy-start.1
  78.6 5.4 %collective-permute-done.3.refs_4_ = bf16[384,512]{1,0:T(8,128)(2,1)S(1)} collective-permute-done((bf16[384,512]{1,0:T(8,128)(2,1)S(1)}, bf16[384,512]{1,0:T(8,128)(2,1)S(1)}, u32[]{:S(2)}, u32[]{:S(2)}) %collective-permute-start.3) | collective-permute-done | bytes 393248 | tf_op jit(solution)/shard_map/ppermute | solution.py:102
  84.0 0.0 collective-permute-done.10.refs_7_
  84.0 0.0 all-gather.3.cloned.1.call-done
  84.0 0.0 copy-done
  84.0 0.0 copy-done.1
  84.0 11.7 %shard_map.74 = f32[1792,512]{1,0:T(8,128)} custom-call(s32[2]{0:T(128)S(1)} %pad_add_fusion.place_ref, bf16[3072,1792]{1,0:T(8,128)(2,1)} %bitcast.18, bf16[384,512]{1,0:T(8,128)(2,1)S(1)} %bitcast.12, bf16[384,512]{1,0:T(8,128)(2,1)S(1)} %collective-permute-done.refs_1_, bf16[384,512]{1,0:T(8,128)(2,1)S(1)} %collective-permute-done.1.refs_2_, ...), custom_call_target="tpu_custom_call" | custom-call | flops 5637144576 | bytes 17825792 | tf_op jit(solution)/shard_map/pallas_call | solution.py:72
Async XLA Ops:
  6.5 77.5 %all-gather.3.cloned.1.call-start = ((), (), s32[]{:S(2)}) async-start(), calls=%async_computation.1 | async-start | bytes 12386304 | tf_op jit(solution)/shard_map/all_gather | solution.py:95
  31.7 6.2 %collective-permute-start.4 = (bf16[384,512]{1,0:T(8,128)(2,1)S(1)}, bf16[384,512]{1,0:T(8,128)(2,1)S(1)}, u32[]{:S(2)}, u32[]{:S(2)}) collective-permute-start(bf16[384,512]{1,0:T(8,128)(2,1)S(1)} %bitcast.10), channel_id=1, source_target_pairs={{0,64},{64,0},{128,192},{192,128},{256,320},{320,256},{384,448},{4... | collective-permute-start | bytes 1179656 | tf_op jit(solution)/shard_map/ppermute | solution.py:105
  33.6 16.7 %collective-permute-start = (bf16[384,512]{1,0:T(8,128)(2,1)S(1)}, bf16[384,512]{1,0:T(8,128)(2,1)S(1)}, u32[]{:S(2)}, u32[]{:S(2)}) collective-permute-start(bf16[384,512]{1,0:T(8,128)(2,1)S(1)} %bitcast.11), channel_id=1, source_target_pairs={{0,8},{8,16},{16,24},{24,32},{32,40},{40,48},{48,56},{56,0},{64,12... | collective-permute-start | bytes 1179656 | tf_op jit(solution)/shard_map/ppermute | solution.py:102
  37.9 16.6 %collective-permute-start.5 = (bf16[384,512]{1,0:T(8,128)(2,1)S(1)}, bf16[384,512]{1,0:T(8,128)(2,1)S(1)}, u32[]{:S(2)}, u32[]{:S(2)}) collective-permute-start(bf16[384,512]{1,0:T(8,128)(2,1)S(1)} %collective-permute-done.4), channel_id=1, source_target_pairs={{0,8},{8,16},{16,24},{24,32},{32,40},{40,48},{48,56},{56,0},{64,12... | collective-permute-start | bytes 1179656 | tf_op jit(solution)/shard_map/ppermute | solution.py:102
  50.3 10.9 %collective-permute-start.1 = (bf16[384,512]{1,0:T(8,128)(2,1)S(1)}, bf16[384,512]{1,0:T(8,128)(2,1)S(1)}, u32[]{:S(2)}, u32[]{:S(2)}) collective-permute-start(bf16[384,512]{1,0:T(8,128)(2,1)S(1)} %collective-permute-done.refs_1_), channel_id=1, source_target_pairs={{0,8},{8,16},{16,24},{24,32},{32,40},{40,48},{48,56},{56,0},{64,12... | collective-permute-start | bytes 1179656 | tf_op jit(solution)/shard_map/ppermute | solution.py:102
  54.6 10.9 %collective-permute-start.7 = (bf16[384,512]{1,0:T(8,128)(2,1)S(1)}, bf16[384,512]{1,0:T(8,128)(2,1)S(1)}, u32[]{:S(2)}, u32[]{:S(2)}) collective-permute-start(bf16[384,512]{1,0:T(8,128)(2,1)S(1)} %collective-permute-done.5), channel_id=1, source_target_pairs={{0,8},{8,16},{16,24},{24,32},{32,40},{40,48},{48,56},{56,0},{64,12... | collective-permute-start | bytes 1179656 | tf_op jit(solution)/shard_map/ppermute | solution.py:102
  61.2 11.9 %collective-permute-start.2 = (bf16[384,512]{1,0:T(8,128)(2,1)S(1)}, bf16[384,512]{1,0:T(8,128)(2,1)S(1)}, u32[]{:S(2)}, u32[]{:S(2)}) collective-permute-start(bf16[384,512]{1,0:T(8,128)(2,1)S(1)} %collective-permute-done.1.refs_2_), channel_id=1, source_target_pairs={{0,8},{8,16},{16,24},{24,32},{32,40},{40,48},{48,56},{56,0},{64,12... | collective-permute-start | bytes 1179656 | tf_op jit(solution)/shard_map/ppermute | solution.py:102
  65.4 11.0 %collective-permute-start.9 = (bf16[384,512]{1,0:T(8,128)(2,1)S(1)}, bf16[384,512]{1,0:T(8,128)(2,1)}, u32[]{:S(2)}, u32[]{:S(2)}) collective-permute-start(bf16[384,512]{1,0:T(8,128)(2,1)S(1)} %collective-permute-done.7), channel_id=1, source_target_pairs={{0,8},{8,16},{16,24},{24,32},{32,40},{40,48},{48,56},{56,0},{64,12... | collective-permute-start | bytes 1179656 | tf_op jit(solution)/shard_map/ppermute | solution.py:102
  67.3 11.2 %collective-permute-start.6 = (bf16[384,512]{1,0:T(8,128)(2,1)S(1)}, bf16[384,512]{1,0:T(8,128)(2,1)S(1)}, u32[]{:S(2)}, u32[]{:S(2)}) collective-permute-start(bf16[384,512]{1,0:T(8,128)(2,1)S(1)} %collective-permute-done.5), channel_id=1, source_target_pairs={{0,64},{64,0},{128,192},{192,128},{256,320},{320,256},{384,448},{4... | collective-permute-start | bytes 1179656 | tf_op jit(solution)/shard_map/ppermute | solution.py:105
  71.2 7.4 %collective-permute-start.8 = (bf16[384,512]{1,0:T(8,128)(2,1)S(1)}, bf16[384,512]{1,0:T(8,128)(2,1)S(1)}, u32[]{:S(2)}, u32[]{:S(2)}) collective-permute-start(bf16[384,512]{1,0:T(8,128)(2,1)S(1)} %collective-permute-done.7), channel_id=1, source_target_pairs={{0,64},{64,0},{128,192},{192,128},{256,320},{320,256},{384,448},{4... | collective-permute-start | bytes 1179656 | tf_op jit(solution)/shard_map/ppermute | solution.py:105
  73.1 10.9 %collective-permute-start.3 = (bf16[384,512]{1,0:T(8,128)(2,1)S(1)}, bf16[384,512]{1,0:T(8,128)(2,1)S(1)}, u32[]{:S(2)}, u32[]{:S(2)}) collective-permute-start(bf16[384,512]{1,0:T(8,128)(2,1)S(1)} %collective-permute-done.2.refs_3_), channel_id=1, source_target_pairs={{0,8},{8,16},{16,24},{24,32},{32,40},{40,48},{48,56},{56,0},{64,12... | collective-permute-start | bytes 1179656 | tf_op jit(solution)/shard_map/ppermute | solution.py:102
  76.4 7.6 %collective-permute-start.10 = (bf16[384,512]{1,0:T(8,128)(2,1)}, bf16[384,512]{1,0:T(8,128)(2,1)}, u32[]{:S(2)}, u32[]{:S(2)}) collective-permute-start(bf16[384,512]{1,0:T(8,128)(2,1)} %collective-permute-done.9), channel_id=1, source_target_pairs={{0,64},{64,0},{128,192},{192,128},{256,320},{320,256},{384,448},{4... | collective-permute-start | bytes 1179656 | tf_op jit(solution)/shard_map/ppermute | solution.py:105
  78.6 5.4 %copy-start = (bf16[384,512]{1,0:T(8,128)(2,1)}, bf16[384,512]{1,0:T(8,128)(2,1)S(1)}, u32[]{:S(2)}) copy-start(bf16[384,512]{1,0:T(8,128)(2,1)S(1)} %collective-permute-done.6.refs_5_) | copy-start | bytes 1179652
  78.6 5.4 %copy-start.1 = (bf16[384,512]{1,0:T(8,128)(2,1)}, bf16[384,512]{1,0:T(8,128)(2,1)S(1)}, u32[]{:S(2)}) copy-start(bf16[384,512]{1,0:T(8,128)(2,1)S(1)} %collective-permute-done.8.refs_6_) | copy-start | bytes 1179652
Sparse Core Ops, SparseCore 0:
  9.5 68.8 all-gather.2

commit v3 on v2

--- a/solution.py
+++ b/solution.py
@@ -8,7 +8,7 @@
 from jax.sharding import PartitionSpec as P
 
 retain_weight = 2.0
-tile = 256
+tile = 896
 
 
 def rows_kernel(lo_ref, fr_ref, control_ref, kind_ref, ids_ref, weights_ref, out_ref, *, experts, scale):
@@ -104,11 +104,16 @@
     def other_core(part):
         return lax.ppermute(part, "rep", cores)
 
+    def after(part, *earlier):
+        return lax.optimization_barrier((part,) + earlier)[0]
+
     ours1, pair0 = next_dp(mine), other_core(mine)
     pair1, ours2 = next_dp(pair0), next_dp(ours1)
-    back1, pair2, ours3 = other_core(pair1), next_dp(pair1), next_dp(ours2)
-    back2, pair3, ours4 = other_core(pair2), next_dp(pair2), next_dp(ours3)
-    back3 = other_core(pair3)
+    back1 = other_core(after(pair1, ours2))
+    pair2, ours3 = next_dp(pair1), next_dp(ours2)
+    back2 = other_core(after(pair2, ours3))
+    pair3, ours4 = next_dp(pair2), next_dp(after(ours3, back1))
+    back3 = other_core(after(pair3, ours3))
     pieces = [mine, ours1, ours2, ours3, ours4, back1, back2, back3]
 
     place = jnp.stack([lax.axis_index("rep"), lax.axis_index("dp")]).astype(jnp.int32)

time: 103 us -> 101 us (0.981)
  waiting for transfers between devices: 24.9 us -> 22.9 us
  Pallas kernels: 14.4 us -> 13.1 us
    ppermute x7, waiting for transfers between devices: 24.2 us -> 22.2 us  [next_dp(): return lax.ppermute(part, ('rep', 'dp'), round_dp)]
    pallas_call x1, Pallas kernels: 11.7 us -> 10.4 us  [product(): pl.pallas_call(product_kernel, grid=(width // tile,), in_specs=in_specs,...]
where the time goes in v3:
time: 101 us
  starting transfers between devices  28.9 us (29%)
  waiting for transfers between devices  22.9 us (23%)
  blocking collectives  21.8 us (22%)
  between operations  13.5 us (13%)
  Pallas kernels  13.1 us (13%)
    ppermute x7, waiting for transfers between devices, next_dp(): return lax.ppermute(part, ('rep', 'dp'), round_dp)  22.2 us
    all_to_all x1, blocking collectives, body(): lax.all_to_all(grad_send, 'expert', split_axis=0, concat_axis=0, tiled=True)  21.8 us
    ppermute x7, starting transfers between devices, next_dp(): return lax.ppermute(part, ('rep', 'dp'), round_dp)  18.1 us
    ppermute x4, starting transfers between devices, other_core(): return lax.ppermute(part, 'rep', cores)  10.7 us
    pallas_call x1, Pallas kernels, product(): pl.pallas_call(product_kernel, grid=(width // tile,), in_specs=in_specs,...  10.4 us
    pallas_call x1, Pallas kernels, outgoing_rows(): pl.pallas_call(lambda *refs: rows_kernel(*refs, experts=experts_all, scal...  2.68 us
  transfers between devices with their start and end apart: 12, of which 6 were waited for; matrix products, arithmetic and copies ran while one was open for 0% of the time, Pallas kernels for 3%

profile of v3, /device:TPU:6, one launch (start us, length us, event | category | flops | bytes accessed | tf_op | source)
XLA Modules:
  0.0 100.9 jit_solution(2643277578665149873)
XLA Ops:
  6.5 0.0 all-gather.3.cloned.1.call-start
  6.5 0.7 all-gather.3.cloned.1.call-update
  7.3 2.7 %shard_map.73 = bf16[384,512]{1,0:T(8,128)(2,1)} custom-call(bf16[128,512]{1,0:T(8,128)(2,1)} %refs_0_.1, bf16[128,512]{1,0:T(8,128)(2,1)} %refs_1_.1, f32[1,512]{1,0:T(1,128)} %bitcast.14, s32[1,128]{1,0:T(1,128)} %bitcast.17, s32[2,128]{1,0:T(2,128)} %bitcast.15, f32[2,128]{1,0:T(2,128)} %bitcast.16), custom_call_target="tpu_custom_call" | custom-call | tf_op jit(solution)/shard_map/pallas_call | solution.py:41
  9.9 21.8 %all_to_all.5 = bf16[8,48,512]{2,1,0:T(8,128)(2,1)S(1)} all-to-all(bf16[8,48,512]{2,1,0:T(8,128)(2,1)} %bitcast.13), channel_id=1, replica_groups=mesh['rep'=8,'dp'=8,'expert'=8] {'expert'}, dimensions={0} | all-to-all | bytes 786432 | tf_op jit(solution)/shard_map/all_to_all | solution.py:96
  31.7 1.9 %collective-permute-start.3 = (bf16[384,512]{1,0:T(8,128)(2,1)S(1)}, bf16[384,512]{1,0:T(8,128)(2,1)S(1)}, u32[]{:S(2)}, u32[]{:S(2)}) collective-permute-start(bf16[384,512]{1,0:T(8,128)(2,1)S(1)} %bitcast.10), channel_id=1, source_target_pairs={{0,64},{64,0},{128,192},{192,128},{256,320},{320,256},{384,448},{4... | collective-permute-start | bytes 1179656 | tf_op jit(solution)/shard_map/ppermute | solution.py:105
  33.6 4.3 %collective-permute-start = (bf16[384,512]{1,0:T(8,128)(2,1)S(1)}, bf16[384,512]{1,0:T(8,128)(2,1)S(1)}, u32[]{:S(2)}, u32[]{:S(2)}) collective-permute-start(bf16[384,512]{1,0:T(8,128)(2,1)S(1)} %bitcast.11), channel_id=1, source_target_pairs={{0,8},{8,16},{16,24},{24,32},{32,40},{40,48},{48,56},{56,0},{64,12... | collective-permute-start | bytes 1179656 | tf_op jit(solution)/shard_map/ppermute | solution.py:102
  37.9 0.0 collective-permute-done.3
  37.9 4.3 %collective-permute-start.4 = (bf16[384,512]{1,0:T(8,128)(2,1)S(1)}, bf16[384,512]{1,0:T(8,128)(2,1)S(1)}, u32[]{:S(2)}, u32[]{:S(2)}) collective-permute-start(bf16[384,512]{1,0:T(8,128)(2,1)S(1)} %collective-permute-done.3), channel_id=1, source_target_pairs={{0,8},{8,16},{16,24},{24,32},{32,40},{40,48},{48,56},{56,0},{64,12... | collective-permute-start | bytes 1179656 | tf_op jit(solution)/shard_map/ppermute | solution.py:102
  42.2 8.1 %collective-permute-done.refs_1_ = bf16[384,512]{1,0:T(8,128)(2,1)S(1)} collective-permute-done((bf16[384,512]{1,0:T(8,128)(2,1)S(1)}, bf16[384,512]{1,0:T(8,128)(2,1)S(1)}, u32[]{:S(2)}, u32[]{:S(2)}) %collective-permute-start) | collective-permute-done | bytes 393248 | tf_op jit(solution)/shard_map/ppermute | solution.py:102
  50.3 1.9 %collective-permute-start.1 = (bf16[384,512]{1,0:T(8,128)(2,1)S(1)}, bf16[384,512]{1,0:T(8,128)(2,1)S(1)}, u32[]{:S(2)}, u32[]{:S(2)}) collective-permute-start(bf16[384,512]{1,0:T(8,128)(2,1)S(1)} %collective-permute-done.refs_1_), channel_id=1, source_target_pairs={{0,8},{8,16},{16,24},{24,32},{32,40},{40,48},{48,56},{56,0},{64,12... | collective-permute-start | bytes 1179656 | tf_op jit(solution)/shard_map/ppermute | solution.py:102
  52.3 2.3 %collective-permute-done.4 = bf16[384,512]{1,0:T(8,128)(2,1)S(1)} collective-permute-done((bf16[384,512]{1,0:T(8,128)(2,1)S(1)}, bf16[384,512]{1,0:T(8,128)(2,1)S(1)}, u32[]{:S(2)}, u32[]{:S(2)}) %collective-permute-start.4) | collective-permute-done | bytes 393248 | tf_op jit(solution)/shard_map/ppermute | solution.py:102
  54.6 1.9 %collective-permute-start.7 = (bf16[384,512]{1,0:T(8,128)(2,1)S(1)}, bf16[384,512]{1,0:T(8,128)(2,1)S(1)}, u32[]{:S(2)}, u32[]{:S(2)}) collective-permute-start(bf16[384,512]{1,0:T(8,128)(2,1)S(1)} %collective-permute-done.4), channel_id=1, source_target_pairs={{0,8},{8,16},{16,24},{24,32},{32,40},{40,48},{48,56},{56,0},{64,12... | collective-permute-start | bytes 1179656 | tf_op jit(solution)/shard_map/ppermute | solution.py:102
  56.5 4.7 %collective-permute-done.1.refs_2_ = bf16[384,512]{1,0:T(8,128)(2,1)S(1)} collective-permute-done((bf16[384,512]{1,0:T(8,128)(2,1)S(1)}, bf16[384,512]{1,0:T(8,128)(2,1)S(1)}, u32[]{:S(2)}, u32[]{:S(2)}) %collective-permute-start.1) | collective-permute-done | bytes 393248 | tf_op jit(solution)/shard_map/ppermute | solution.py:102
  61.2 1.9 %collective-permute-start.2 = (bf16[384,512]{1,0:T(8,128)(2,1)S(1)}, bf16[384,512]{1,0:T(8,128)(2,1)S(1)}, u32[]{:S(2)}, u32[]{:S(2)}) collective-permute-start(bf16[384,512]{1,0:T(8,128)(2,1)S(1)} %collective-permute-done.1.refs_2_), channel_id=1, source_target_pairs={{0,8},{8,16},{16,24},{24,32},{32,40},{40,48},{48,56},{56,0},{64,12... | collective-permute-start | bytes 1179656 | tf_op jit(solution)/shard_map/ppermute | solution.py:102
  63.1 3.8 %collective-permute-start.5 = (bf16[384,512]{1,0:T(8,128)(2,1)S(1)}, bf16[384,512]{1,0:T(8,128)(2,1)S(1)}, u32[]{:S(2)}, u32[]{:S(2)}) collective-permute-start(bf16[384,512]{1,0:T(8,128)(2,1)S(1)} %collective-permute-done.4), channel_id=1, source_target_pairs={{0,64},{64,0},{128,192},{192,128},{256,320},{320,256},{384,448},{4... | collective-permute-start | bytes 1179656 | tf_op jit(solution)/shard_map/ppermute | solution.py:105
  67.0 0.0 collective-permute-done.7
  67.0 1.9 %collective-permute-start.9 = (bf16[384,512]{1,0:T(8,128)(2,1)S(1)}, bf16[384,512]{1,0:T(8,128)(2,1)S(1)}, u32[]{:S(2)}, u32[]{:S(2)}) collective-permute-start(bf16[384,512]{1,0:T(8,128)(2,1)S(1)} %collective-permute-done.7), channel_id=1, source_target_pairs={{0,8},{8,16},{16,24},{24,32},{32,40},{40,48},{48,56},{56,0},{64,12... | collective-permute-start | bytes 1179656 | tf_op jit(solution)/shard_map/ppermute | solution.py:102
  68.9 3.2 %collective-permute-done.2.refs_3_ = bf16[384,512]{1,0:T(8,128)(2,1)S(1)} collective-permute-done((bf16[384,512]{1,0:T(8,128)(2,1)S(1)}, bf16[384,512]{1,0:T(8,128)(2,1)S(1)}, u32[]{:S(2)}, u32[]{:S(2)}) %collective-permute-start.2) | collective-permute-done | bytes 393248 | tf_op jit(solution)/shard_map/ppermute | solution.py:102
  72.1 0.0 collective-permute-done.5.refs_5_
  72.1 0.0 copy-start
  72.1 1.9 %collective-permute-start.6 = (bf16[384,512]{1,0:T(8,128)(2,1)S(1)}, bf16[384,512]{1,0:T(8,128)(2,1)S(1)}, u32[]{:S(2)}, u32[]{:S(2)}) collective-permute-start(bf16[384,512]{1,0:T(8,128)(2,1)S(1)} %collective-permute-done.2.refs_3_), channel_id=1, source_target_pairs={{0,8},{8,16},{16,24},{24,32},{32,40},{40,48},{48,56},{56,0},{64,12... | collective-permute-start | bytes 1179656 | tf_op jit(solution)/shard_map/ppermute | solution.py:102
  74.0 3.1 %collective-permute-start.8 = (bf16[384,512]{1,0:T(8,128)(2,1)S(1)}, bf16[384,512]{1,0:T(8,128)(2,1)S(1)}, u32[]{:S(2)}, u32[]{:S(2)}) collective-permute-start(bf16[384,512]{1,0:T(8,128)(2,1)S(1)} %collective-permute-done.7), channel_id=1, source_target_pairs={{0,64},{64,0},{128,192},{192,128},{256,320},{320,256},{384,448},{4... | collective-permute-start | bytes 1179656 | tf_op jit(solution)/shard_map/ppermute | solution.py:105
  77.1 0.8 collective-permute-done.9
  77.9 1.9 %collective-permute-start.10 = (bf16[384,512]{1,0:T(8,128)(2,1)S(1)}, bf16[384,512]{1,0:T(8,128)(2,1)}, u32[]{:S(2)}, u32[]{:S(2)}) collective-permute-start(bf16[384,512]{1,0:T(8,128)(2,1)S(1)} %collective-permute-done.9), channel_id=1, source_target_pairs={{0,64},{64,0},{128,192},{192,128},{256,320},{320,256},{384,448},{4... | collective-permute-start | bytes 1179656 | tf_op jit(solution)/shard_map/ppermute | solution.py:105
  79.8 0.1 pad_add_fusion.place_ref
  79.9 3.1 %collective-permute-done.6.refs_4_ = bf16[384,512]{1,0:T(8,128)(2,1)S(1)} collective-permute-done((bf16[384,512]{1,0:T(8,128)(2,1)S(1)}, bf16[384,512]{1,0:T(8,128)(2,1)S(1)}, u32[]{:S(2)}, u32[]{:S(2)}) %collective-permute-start.6) | collective-permute-done | bytes 393248 | tf_op jit(solution)/shard_map/ppermute | solution.py:102
  83.0 0.0 collective-permute-done.8.refs_6_
  83.0 0.0 copy-start.1
  83.0 0.0 collective-permute-done.10.refs_7_
  83.0 0.0 all-gather.3.cloned.1.call-done
  83.0 0.0 copy-done
  83.0 0.7 copy-done.1
  83.7 10.4 %shard_map.74 = f32[1792,512]{1,0:T(8,128)} custom-call(s32[2]{0:T(128)S(1)} %pad_add_fusion.place_ref, bf16[3072,1792]{1,0:T(8,128)(2,1)} %bitcast.18, bf16[384,512]{1,0:T(8,128)(2,1)S(1)} %bitcast.12, bf16[384,512]{1,0:T(8,128)(2,1)S(1)} %collective-permute-done.refs_1_, bf16[384,512]{1,0:T(8,128)(2,1)S(1)} %collective-permute-done.1.refs_2_, ...), custom_call_target="tpu_custom_call" | custom-call | flops 5637144576 | bytes 17825792 | tf_op jit(solution)/shard_map/pallas_call | solution.py:72
Async XLA Ops:
  6.5 76.5 %all-gather.3.cloned.1.call-start = ((), (), s32[]{:S(2)}) async-start(), calls=%async_computation.1 | async-start | bytes 12386304 | tf_op jit(solution)/shard_map/all_gather | solution.py:95
  31.7 6.2 %collective-permute-start.3 = (bf16[384,512]{1,0:T(8,128)(2,1)S(1)}, bf16[384,512]{1,0:T(8,128)(2,1)S(1)}, u32[]{:S(2)}, u32[]{:S(2)}) collective-permute-start(bf16[384,512]{1,0:T(8,128)(2,1)S(1)} %bitcast.10), channel_id=1, source_target_pairs={{0,64},{64,0},{128,192},{192,128},{256,320},{320,256},{384,448},{4... | collective-permute-start | bytes 1179656 | tf_op jit(solution)/shard_map/ppermute | solution.py:105
  33.6 16.7 %collective-permute-start = (bf16[384,512]{1,0:T(8,128)(2,1)S(1)}, bf16[384,512]{1,0:T(8,128)(2,1)S(1)}, u32[]{:S(2)}, u32[]{:S(2)}) collective-permute-start(bf16[384,512]{1,0:T(8,128)(2,1)S(1)} %bitcast.11), channel_id=1, source_target_pairs={{0,8},{8,16},{16,24},{24,32},{32,40},{40,48},{48,56},{56,0},{64,12... | collective-permute-start | bytes 1179656 | tf_op jit(solution)/shard_map/ppermute | solution.py:102
  37.9 16.6 %collective-permute-start.4 = (bf16[384,512]{1,0:T(8,128)(2,1)S(1)}, bf16[384,512]{1,0:T(8,128)(2,1)S(1)}, u32[]{:S(2)}, u32[]{:S(2)}) collective-permute-start(bf16[384,512]{1,0:T(8,128)(2,1)S(1)} %collective-permute-done.3), channel_id=1, source_target_pairs={{0,8},{8,16},{16,24},{24,32},{32,40},{40,48},{48,56},{56,0},{64,12... | collective-permute-start | bytes 1179656 | tf_op jit(solution)/shard_map/ppermute | solution.py:102
  50.3 10.9 %collective-permute-start.1 = (bf16[384,512]{1,0:T(8,128)(2,1)S(1)}, bf16[384,512]{1,0:T(8,128)(2,1)S(1)}, u32[]{:S(2)}, u32[]{:S(2)}) collective-permute-start(bf16[384,512]{1,0:T(8,128)(2,1)S(1)} %collective-permute-done.refs_1_), channel_id=1, source_target_pairs={{0,8},{8,16},{16,24},{24,32},{32,40},{40,48},{48,56},{56,0},{64,12... | collective-permute-start | bytes 1179656 | tf_op jit(solution)/shard_map/ppermute | solution.py:102
  54.6 12.4 %collective-permute-start.7 = (bf16[384,512]{1,0:T(8,128)(2,1)S(1)}, bf16[384,512]{1,0:T(8,128)(2,1)S(1)}, u32[]{:S(2)}, u32[]{:S(2)}) collective-permute-start(bf16[384,512]{1,0:T(8,128)(2,1)S(1)} %collective-permute-done.4), channel_id=1, source_target_pairs={{0,8},{8,16},{16,24},{24,32},{32,40},{40,48},{48,56},{56,0},{64,12... | collective-permute-start | bytes 1179656 | tf_op jit(solution)/shard_map/ppermute | solution.py:102
  61.2 10.9 %collective-permute-start.2 = (bf16[384,512]{1,0:T(8,128)(2,1)S(1)}, bf16[384,512]{1,0:T(8,128)(2,1)S(1)}, u32[]{:S(2)}, u32[]{:S(2)}) collective-permute-start(bf16[384,512]{1,0:T(8,128)(2,1)S(1)} %collective-permute-done.1.refs_2_), channel_id=1, source_target_pairs={{0,8},{8,16},{16,24},{24,32},{32,40},{40,48},{48,56},{56,0},{64,12... | collective-permute-start | bytes 1179656 | tf_op jit(solution)/shard_map/ppermute | solution.py:102
  63.1 9.0 %collective-permute-start.5 = (bf16[384,512]{1,0:T(8,128)(2,1)S(1)}, bf16[384,512]{1,0:T(8,128)(2,1)S(1)}, u32[]{:S(2)}, u32[]{:S(2)}) collective-permute-start(bf16[384,512]{1,0:T(8,128)(2,1)S(1)} %collective-permute-done.4), channel_id=1, source_target_pairs={{0,64},{64,0},{128,192},{192,128},{256,320},{320,256},{384,448},{4... | collective-permute-start | bytes 1179656 | tf_op jit(solution)/shard_map/ppermute | solution.py:105
  67.0 10.9 %collective-permute-start.9 = (bf16[384,512]{1,0:T(8,128)(2,1)S(1)}, bf16[384,512]{1,0:T(8,128)(2,1)S(1)}, u32[]{:S(2)}, u32[]{:S(2)}) collective-permute-start(bf16[384,512]{1,0:T(8,128)(2,1)S(1)} %collective-permute-done.7), channel_id=1, source_target_pairs={{0,8},{8,16},{16,24},{24,32},{32,40},{40,48},{48,56},{56,0},{64,12... | collective-permute-start | bytes 1179656 | tf_op jit(solution)/shard_map/ppermute | solution.py:102
  72.1 10.9 %copy-start = (bf16[384,512]{1,0:T(8,128)(2,1)}, bf16[384,512]{1,0:T(8,128)(2,1)S(1)}, u32[]{:S(2)}) copy-start(bf16[384,512]{1,0:T(8,128)(2,1)S(1)} %collective-permute-done.5.refs_5_) | copy-start | bytes 1179652
  72.1 10.9 %collective-permute-start.6 = (bf16[384,512]{1,0:T(8,128)(2,1)S(1)}, bf16[384,512]{1,0:T(8,128)(2,1)S(1)}, u32[]{:S(2)}, u32[]{:S(2)}) collective-permute-start(bf16[384,512]{1,0:T(8,128)(2,1)S(1)} %collective-permute-done.2.refs_3_), channel_id=1, source_target_pairs={{0,8},{8,16},{16,24},{24,32},{32,40},{40,48},{48,56},{56,0},{64,12... | collective-permute-start | bytes 1179656 | tf_op jit(solution)/shard_map/ppermute | solution.py:102
  74.0 9.0 %collective-permute-start.8 = (bf16[384,512]{1,0:T(8,128)(2,1)S(1)}, bf16[384,512]{1,0:T(8,128)(2,1)S(1)}, u32[]{:S(2)}, u32[]{:S(2)}) collective-permute-start(bf16[384,512]{1,0:T(8,128)(2,1)S(1)} %collective-permute-done.7), channel_id=1, source_target_pairs={{0,64},{64,0},{128,192},{192,128},{256,320},{320,256},{384,448},{4... | collective-permute-start | bytes 1179656 | tf_op jit(solution)/shard_map/ppermute | solution.py:105
  77.9 5.1 %collective-permute-start.10 = (bf16[384,512]{1,0:T(8,128)(2,1)S(1)}, bf16[384,512]{1,0:T(8,128)(2,1)}, u32[]{:S(2)}, u32[]{:S(2)}) collective-permute-start(bf16[384,512]{1,0:T(8,128)(2,1)S(1)} %collective-permute-done.9), channel_id=1, source_target_pairs={{0,64},{64,0},{128,192},{192,128},{256,320},{320,256},{384,448},{4... | collective-permute-start | bytes 1179656 | tf_op jit(solution)/shard_map/ppermute | solution.py:105
  83.0 0.7 copy-start.1
Sparse Core Ops, SparseCore 0:
  9.5 69.0 all-gather.2

commit v4 on v3

--- a/solution.py
+++ b/solution.py
@@ -107,13 +107,16 @@
     def after(part, *earlier):
         return lax.optimization_barrier((part,) + earlier)[0]
 
-    ours1, pair0 = next_dp(mine), other_core(mine)
-    pair1, ours2 = next_dp(pair0), next_dp(ours1)
+    def crossing(part, way):
+        pairs = [(r * 8 + d, (r ^ 1) * 8 + (d + (way, -way)[r % 2]) % 8) for r in range(8) for d in range(8)]
+        return lax.ppermute(part, ("rep", "dp"), pairs)
+
+    ours1, pair1 = next_dp(mine), crossing(mine, -1)
+    ours2, pair2 = next_dp(ours1), next_dp(pair1)
     back1 = other_core(after(pair1, ours2))
-    pair2, ours3 = next_dp(pair1), next_dp(ours2)
+    ours3, back3 = next_dp(ours2), crossing(pair2, 1)
+    ours4 = next_dp(after(ours3, back1))
     back2 = other_core(after(pair2, ours3))
-    pair3, ours4 = next_dp(pair2), next_dp(after(ours3, back1))
-    back3 = other_core(after(pair3, ours3))
     pieces = [mine, ours1, ours2, ours3, ours4, back1, back2, back3]
 
     place = jnp.stack([lax.axis_index("rep"), lax.axis_index("dp")]).astype(jnp.int32)

time: 101 us -> 104 us (1.030)
  waiting for transfers between devices: 22.9 us -> 29.4 us
  starting transfers between devices: 28.9 us -> 24.5 us
    ppermute x0 -> x2, starting transfers between devices: none -> 8.74 us  [crossing(): return lax.ppermute(part, ('rep', 'dp'), pairs)]
    ppermute x4 -> x2, starting transfers between devices: 10.7 us -> 3.84 us  [other_core(): return lax.ppermute(part, 'rep', cores)]
    ppermute x7 -> x5, waiting for transfers between devices: 22.2 us -> 28.7 us  [next_dp(): return lax.ppermute(part, ('rep', 'dp'), round_dp)]
    ppermute x7 -> x5, starting transfers between devices: 18.1 us -> 11.9 us  [next_dp(): return lax.ppermute(part, ('rep', 'dp'), round_dp)]
  transfers between devices with their start and end apart: 12 -> 10, of which waited for: 6 -> 5; matrix products, arithmetic and copies ran while one was open for 0% -> 0% of each run, Pallas kernels for 3% -> 3%
where the time goes in v4:
time: 104 us; the launch traced here: 103 us
  waiting for transfers between devices  29.4 us (28%)
  starting transfers between devices  24.5 us (24%)
  blocking collectives  21.8 us (21%)
  between operations  13.5 us (13%)
  Pallas kernels  13.1 us (13%)
    ppermute x5, waiting for transfers between devices, next_dp(): return lax.ppermute(part, ('rep', 'dp'), round_dp)  28.7 us
    all_to_all x1, blocking collectives, body(): lax.all_to_all(grad_send, 'expert', split_axis=0, concat_axis=0, tiled=True)  21.8 us
    ppermute x5, starting transfers between devices, next_dp(): return lax.ppermute(part, ('rep', 'dp'), round_dp)  11.9 us
    pallas_call x1, Pallas kernels, product(): pl.pallas_call(product_kernel, grid=(width // tile,), in_specs=in_specs,...  10.4 us
    ppermute x2, starting transfers between devices, crossing(): return lax.ppermute(part, ('rep', 'dp'), pairs)  8.74 us
    ppermute x2, starting transfers between devices, other_core(): return lax.ppermute(part, 'rep', cores)  3.84 us
    pallas_call x1, Pallas kernels, outgoing_rows(): pl.pallas_call(lambda *refs: rows_kernel(*refs, experts=experts_all, scal...  2.68 us
  transfers between devices with their start and end apart: 10, of which 5 were waited for; matrix products, arithmetic and copies ran while one was open for 0% of the time, Pallas kernels for 3%

profile of v4, /device:TPU:6, one launch (start us, length us, event | category | flops | bytes accessed | tf_op | source)
XLA Modules:
  0.0 103.1 jit_solution(2097120959611022029)
XLA Ops:
  6.5 0.0 all-gather.3.cloned.1.call-start
  6.5 0.7 all-gather.3.cloned.1.call-update
  7.3 2.7 %shard_map.73 = bf16[384,512]{1,0:T(8,128)(2,1)} custom-call(bf16[128,512]{1,0:T(8,128)(2,1)} %refs_0_.1, bf16[128,512]{1,0:T(8,128)(2,1)} %refs_1_.1, f32[1,512]{1,0:T(1,128)} %bitcast.14, s32[1,128]{1,0:T(1,128)} %bitcast.17, s32[2,128]{1,0:T(2,128)} %bitcast.15, f32[2,128]{1,0:T(2,128)} %bitcast.16), custom_call_target="tpu_custom_call" | custom-call | tf_op jit(solution)/shard_map/pallas_call | solution.py:41
  9.9 21.8 %all_to_all.5 = bf16[8,48,512]{2,1,0:T(8,128)(2,1)S(1)} all-to-all(bf16[8,48,512]{2,1,0:T(8,128)(2,1)} %bitcast.13), channel_id=1, replica_groups=mesh['rep'=8,'dp'=8,'expert'=8] {'expert'}, dimensions={0} | all-to-all | bytes 786432 | tf_op jit(solution)/shard_map/all_to_all | solution.py:96
  31.7 4.3 %collective-permute-start = (bf16[384,512]{1,0:T(8,128)(2,1)S(1)}, bf16[384,512]{1,0:T(8,128)(2,1)S(1)}, u32[]{:S(2)}, u32[]{:S(2)}) collective-permute-start(bf16[384,512]{1,0:T(8,128)(2,1)S(1)} %bitcast.10), channel_id=1, source_target_pairs={{0,8},{8,16},{16,24},{24,32},{32,40},{40,48},{48,56},{56,0},{64,12... | collective-permute-start | bytes 1179656 | tf_op jit(solution)/shard_map/ppermute | solution.py:102
  36.0 6.8 %collective-permute-start.3 = (bf16[384,512]{1,0:T(8,128)(2,1)S(1)}, bf16[384,512]{1,0:T(8,128)(2,1)S(1)}, u32[]{:S(2)}, u32[]{:S(2)}) collective-permute-start(bf16[384,512]{1,0:T(8,128)(2,1)S(1)} %bitcast.11), channel_id=1, source_target_pairs={{0,120},{8,64},{16,72},{24,80},{32,88},{40,96},{48,104},{56,112},{... | collective-permute-start | bytes 1179656 | tf_op jit(solution)/shard_map/ppermute | solution.py:112
  42.8 9.7 %collective-permute-done.refs_1_ = bf16[384,512]{1,0:T(8,128)(2,1)S(1)} collective-permute-done((bf16[384,512]{1,0:T(8,128)(2,1)S(1)}, bf16[384,512]{1,0:T(8,128)(2,1)S(1)}, u32[]{:S(2)}, u32[]{:S(2)}) %collective-permute-start) | collective-permute-done | bytes 393248 | tf_op jit(solution)/shard_map/ppermute | solution.py:102
  52.5 1.9 %collective-permute-start.1 = (bf16[384,512]{1,0:T(8,128)(2,1)S(1)}, bf16[384,512]{1,0:T(8,128)(2,1)S(1)}, u32[]{:S(2)}, u32[]{:S(2)}) collective-permute-start(bf16[384,512]{1,0:T(8,128)(2,1)S(1)} %collective-permute-done.refs_1_), channel_id=1, source_target_pairs={{0,8},{8,16},{16,24},{24,32},{32,40},{40,48},{48,56},{56,0},{64,12... | collective-permute-start | bytes 1179656 | tf_op jit(solution)/shard_map/ppermute | solution.py:102
  54.4 0.0 collective-permute-done.3
  54.4 1.9 %collective-permute-start.6 = (bf16[384,512]{1,0:T(8,128)(2,1)S(1)}, bf16[384,512]{1,0:T(8,128)(2,1)S(1)}, u32[]{:S(2)}, u32[]{:S(2)}) collective-permute-start(bf16[384,512]{1,0:T(8,128)(2,1)S(1)} %collective-permute-done.3), channel_id=1, source_target_pairs={{0,8},{8,16},{16,24},{24,32},{32,40},{40,48},{48,56},{56,0},{64,12... | collective-permute-start | bytes 1179656 | tf_op jit(solution)/shard_map/ppermute | solution.py:102
  56.4 7.0 %collective-permute-done.1.refs_2_ = bf16[384,512]{1,0:T(8,128)(2,1)S(1)} collective-permute-done((bf16[384,512]{1,0:T(8,128)(2,1)S(1)}, bf16[384,512]{1,0:T(8,128)(2,1)S(1)}, u32[]{:S(2)}, u32[]{:S(2)}) %collective-permute-start.1) | collective-permute-done | bytes 393248 | tf_op jit(solution)/shard_map/ppermute | solution.py:102
  63.4 1.9 %collective-permute-start.2 = (bf16[384,512]{1,0:T(8,128)(2,1)S(1)}, bf16[384,512]{1,0:T(8,128)(2,1)S(1)}, u32[]{:S(2)}, u32[]{:S(2)}) collective-permute-start(bf16[384,512]{1,0:T(8,128)(2,1)S(1)} %collective-permute-done.1.refs_2_), channel_id=1, source_target_pairs={{0,8},{8,16},{16,24},{24,32},{32,40},{40,48},{48,56},{56,0},{64,12... | collective-permute-start | bytes 1179656 | tf_op jit(solution)/shard_map/ppermute | solution.py:102
  65.3 1.9 %collective-permute-start.4 = (bf16[384,512]{1,0:T(8,128)(2,1)S(1)}, bf16[384,512]{1,0:T(8,128)(2,1)S(1)}, u32[]{:S(2)}, u32[]{:S(2)}) collective-permute-start(bf16[384,512]{1,0:T(8,128)(2,1)S(1)} %collective-permute-done.3), channel_id=1, source_target_pairs={{0,64},{64,0},{128,192},{192,128},{256,320},{320,256},{384,448},{4... | collective-permute-start | bytes 1179656 | tf_op jit(solution)/shard_map/ppermute | solution.py:105
  67.2 0.4 collective-permute-done.6
  67.6 1.9 %collective-permute-start.8 = (bf16[384,512]{1,0:T(8,128)(2,1)S(1)}, bf16[384,512]{1,0:T(8,128)(2,1)S(1)}, u32[]{:S(2)}, u32[]{:S(2)}) collective-permute-start(bf16[384,512]{1,0:T(8,128)(2,1)S(1)} %collective-permute-done.6), channel_id=1, source_target_pairs={{0,72},{8,80},{16,88},{24,96},{32,104},{40,112},{48,120},{56,64},{... | collective-permute-start | bytes 1179656 | tf_op jit(solution)/shard_map/ppermute | solution.py:112
  69.5 4.7 %collective-permute-done.2.refs_3_ = bf16[384,512]{1,0:T(8,128)(2,1)S(1)} collective-permute-done((bf16[384,512]{1,0:T(8,128)(2,1)S(1)}, bf16[384,512]{1,0:T(8,128)(2,1)S(1)}, u32[]{:S(2)}, u32[]{:S(2)}) %collective-permute-start.2) | collective-permute-done | bytes 393248 | tf_op jit(solution)/shard_map/ppermute | solution.py:102
  74.2 0.0 collective-permute-done.4.refs_5_
  74.2 0.0 copy-start
  74.2 1.9 %collective-permute-start.5 = (bf16[384,512]{1,0:T(8,128)(2,1)S(1)}, bf16[384,512]{1,0:T(8,128)(2,1)S(1)}, u32[]{:S(2)}, u32[]{:S(2)}) collective-permute-start(bf16[384,512]{1,0:T(8,128)(2,1)S(1)} %collective-permute-done.2.refs_3_), channel_id=1, source_target_pairs={{0,8},{8,16},{16,24},{24,32},{32,40},{40,48},{48,56},{56,0},{64,12... | collective-permute-start | bytes 1179656 | tf_op jit(solution)/shard_map/ppermute | solution.py:102
  76.2 1.9 %collective-permute-start.7 = (bf16[384,512]{1,0:T(8,128)(2,1)S(1)}, bf16[384,512]{1,0:T(8,128)(2,1)S(1)}, u32[]{:S(2)}, u32[]{:S(2)}) collective-permute-start(bf16[384,512]{1,0:T(8,128)(2,1)S(1)} %collective-permute-done.6), channel_id=1, source_target_pairs={{0,64},{64,0},{128,192},{192,128},{256,320},{320,256},{384,448},{4... | collective-permute-start | bytes 1179656 | tf_op jit(solution)/shard_map/ppermute | solution.py:105
  78.1 0.1 pad_add_fusion.place_ref
  78.2 0.0 collective-permute-done.8.refs_7_
  78.2 0.0 copy-start.1
  78.2 6.9 %collective-permute-done.5.refs_4_ = bf16[384,512]{1,0:T(8,128)(2,1)S(1)} collective-permute-done((bf16[384,512]{1,0:T(8,128)(2,1)S(1)}, bf16[384,512]{1,0:T(8,128)(2,1)S(1)}, u32[]{:S(2)}, u32[]{:S(2)}) %collective-permute-start.5) | collective-permute-done | bytes 393248 | tf_op jit(solution)/shard_map/ppermute | solution.py:102
  85.1 0.0 collective-permute-done.7.refs_6_
  85.1 0.0 copy-start.2
  85.1 0.0 all-gather.3.cloned.1.call-done
  85.1 0.0 copy-done
  85.1 0.0 copy-done.1
  85.1 0.7 copy-done.2
  85.9 10.4 %shard_map.74 = f32[1792,512]{1,0:T(8,128)} custom-call(s32[2]{0:T(128)S(1)} %pad_add_fusion.place_ref, bf16[3072,1792]{1,0:T(8,128)(2,1)} %bitcast.18, bf16[384,512]{1,0:T(8,128)(2,1)S(1)} %bitcast.12, bf16[384,512]{1,0:T(8,128)(2,1)S(1)} %collective-permute-done.refs_1_, bf16[384,512]{1,0:T(8,128)(2,1)S(1)} %collective-permute-done.1.refs_2_, ...), custom_call_target="tpu_custom_call" | custom-call | flops 5637144576 | bytes 17825792 | tf_op jit(solution)/shard_map/pallas_call | solution.py:72
Async XLA Ops:
  6.5 78.6 %all-gather.3.cloned.1.call-start = ((), (), s32[]{:S(2)}) async-start(), calls=%async_computation.1 | async-start | bytes 12386304 | tf_op jit(solution)/shard_map/all_gather | solution.py:95
  31.7 20.8 %collective-permute-start = (bf16[384,512]{1,0:T(8,128)(2,1)S(1)}, bf16[384,512]{1,0:T(8,128)(2,1)S(1)}, u32[]{:S(2)}, u32[]{:S(2)}) collective-permute-start(bf16[384,512]{1,0:T(8,128)(2,1)S(1)} %bitcast.10), channel_id=1, source_target_pairs={{0,8},{8,16},{16,24},{24,32},{32,40},{40,48},{48,56},{56,0},{64,12... | collective-permute-start | bytes 1179656 | tf_op jit(solution)/shard_map/ppermute | solution.py:102
  36.0 18.4 %collective-permute-start.3 = (bf16[384,512]{1,0:T(8,128)(2,1)S(1)}, bf16[384,512]{1,0:T(8,128)(2,1)S(1)}, u32[]{:S(2)}, u32[]{:S(2)}) collective-permute-start(bf16[384,512]{1,0:T(8,128)(2,1)S(1)} %bitcast.11), channel_id=1, source_target_pairs={{0,120},{8,64},{16,72},{24,80},{32,88},{40,96},{48,104},{56,112},{... | collective-permute-start | bytes 1179656 | tf_op jit(solution)/shard_map/ppermute | solution.py:112
  52.5 10.9 %collective-permute-start.1 = (bf16[384,512]{1,0:T(8,128)(2,1)S(1)}, bf16[384,512]{1,0:T(8,128)(2,1)S(1)}, u32[]{:S(2)}, u32[]{:S(2)}) collective-permute-start(bf16[384,512]{1,0:T(8,128)(2,1)S(1)} %collective-permute-done.refs_1_), channel_id=1, source_target_pairs={{0,8},{8,16},{16,24},{24,32},{32,40},{40,48},{48,56},{56,0},{64,12... | collective-permute-start | bytes 1179656 | tf_op jit(solution)/shard_map/ppermute | solution.py:102
  54.4 13.2 %collective-permute-start.6 = (bf16[384,512]{1,0:T(8,128)(2,1)S(1)}, bf16[384,512]{1,0:T(8,128)(2,1)S(1)}, u32[]{:S(2)}, u32[]{:S(2)}) collective-permute-start(bf16[384,512]{1,0:T(8,128)(2,1)S(1)} %collective-permute-done.3), channel_id=1, source_target_pairs={{0,8},{8,16},{16,24},{24,32},{32,40},{40,48},{48,56},{56,0},{64,12... | collective-permute-start | bytes 1179656 | tf_op jit(solution)/shard_map/ppermute | solution.py:102
  63.4 10.9 %collective-permute-start.2 = (bf16[384,512]{1,0:T(8,128)(2,1)S(1)}, bf16[384,512]{1,0:T(8,128)(2,1)S(1)}, u32[]{:S(2)}, u32[]{:S(2)}) collective-permute-start(bf16[384,512]{1,0:T(8,128)(2,1)S(1)} %collective-permute-done.1.refs_2_), channel_id=1, source_target_pairs={{0,8},{8,16},{16,24},{24,32},{32,40},{40,48},{48,56},{56,0},{64,12... | collective-permute-start | bytes 1179656 | tf_op jit(solution)/shard_map/ppermute | solution.py:102
  65.3 9.0 %collective-permute-start.4 = (bf16[384,512]{1,0:T(8,128)(2,1)S(1)}, bf16[384,512]{1,0:T(8,128)(2,1)S(1)}, u32[]{:S(2)}, u32[]{:S(2)}) collective-permute-start(bf16[384,512]{1,0:T(8,128)(2,1)S(1)} %collective-permute-done.3), channel_id=1, source_target_pairs={{0,64},{64,0},{128,192},{192,128},{256,320},{320,256},{384,448},{4... | collective-permute-start | bytes 1179656 | tf_op jit(solution)/shard_map/ppermute | solution.py:105
  67.6 10.6 %collective-permute-start.8 = (bf16[384,512]{1,0:T(8,128)(2,1)S(1)}, bf16[384,512]{1,0:T(8,128)(2,1)S(1)}, u32[]{:S(2)}, u32[]{:S(2)}) collective-permute-start(bf16[384,512]{1,0:T(8,128)(2,1)S(1)} %collective-permute-done.6), channel_id=1, source_target_pairs={{0,72},{8,80},{16,88},{24,96},{32,104},{40,112},{48,120},{56,64},{... | collective-permute-start | bytes 1179656 | tf_op jit(solution)/shard_map/ppermute | solution.py:112
  74.2 10.9 %copy-start = (bf16[384,512]{1,0:T(8,128)(2,1)}, bf16[384,512]{1,0:T(8,128)(2,1)S(1)}, u32[]{:S(2)}) copy-start(bf16[384,512]{1,0:T(8,128)(2,1)S(1)} %collective-permute-done.4.refs_5_) | copy-start | bytes 1179652
  74.2 10.9 %collective-permute-start.5 = (bf16[384,512]{1,0:T(8,128)(2,1)S(1)}, bf16[384,512]{1,0:T(8,128)(2,1)S(1)}, u32[]{:S(2)}, u32[]{:S(2)}) collective-permute-start(bf16[384,512]{1,0:T(8,128)(2,1)S(1)} %collective-permute-done.2.refs_3_), channel_id=1, source_target_pairs={{0,8},{8,16},{16,24},{24,32},{32,40},{40,48},{48,56},{56,0},{64,12... | collective-permute-start | bytes 1179656 | tf_op jit(solution)/shard_map/ppermute | solution.py:102
  76.2 9.0 %collective-permute-start.7 = (bf16[384,512]{1,0:T(8,128)(2,1)S(1)}, bf16[384,512]{1,0:T(8,128)(2,1)S(1)}, u32[]{:S(2)}, u32[]{:S(2)}) collective-permute-start(bf16[384,512]{1,0:T(8,128)(2,1)S(1)} %collective-permute-done.6), channel_id=1, source_target_pairs={{0,64},{64,0},{128,192},{192,128},{256,320},{320,256},{384,448},{4... | collective-permute-start | bytes 1179656 | tf_op jit(solution)/shard_map/ppermute | solution.py:105
  78.2 7.0 %copy-start.1 = (bf16[384,512]{1,0:T(8,128)(2,1)}, bf16[384,512]{1,0:T(8,128)(2,1)S(1)}, u32[]{:S(2)}) copy-start(bf16[384,512]{1,0:T(8,128)(2,1)S(1)} %collective-permute-done.8.refs_7_) | copy-start | bytes 1179652
  85.1 0.7 copy-start.2
Sparse Core Ops, SparseCore 0:
  9.5 68.8 all-gather.2

commit v5 on v3

--- a/solution.py
+++ b/solution.py
@@ -24,14 +24,25 @@
     slot = jnp.dot(named, earlier, preferred_element_type=jnp.float32).astype(jnp.int32)
     slot = jnp.where(first | second, slot, -1)
     wanted = lax.broadcasted_iota(jnp.int32, (experts, capacity, tokens), 1)
-    placed = jnp.where(slot[:, None, :] == wanted, weight[:, None, :], 0.0)
-    placed = placed.reshape(experts * capacity, tokens)
+    taken = slot[:, None, :] == wanted
+    scaling = jnp.sum(jnp.where(taken, weight[:, None, :], 0.0), axis=2, keepdims=True)
+    scaling = scaling.reshape(experts * capacity, 1)
+    chosen = jnp.where(taken, 1.0, 0.0).reshape(experts * capacity, tokens).astype(jnp.bfloat16)
     kind = jnp.sum(jnp.where(down == across, kind_ref[...], 0), axis=1, keepdims=True)
     retain = kind == 1
     target = jnp.where(retain, fr_ref[...].astype(jnp.float32), control_ref[...])
     factor = jnp.where(retain, jnp.float32(retain_weight), jnp.float32(1.0))
     out_grad = factor * (lo_ref[...].astype(jnp.float32) - target) * scale
-    rows = jnp.dot(placed, out_grad, precision=lax.Precision.HIGHEST, preferred_element_type=jnp.float32)
+    high = out_grad.astype(jnp.bfloat16)
+    rest = out_grad - high.astype(jnp.float32)
+    middle = rest.astype(jnp.bfloat16)
+    low = (rest - middle.astype(jnp.float32)).astype(jnp.bfloat16)
+    rows = jnp.dot(
+        jnp.concatenate([chosen, chosen, chosen], axis=1),
+        jnp.concatenate([high, middle, low], axis=0),
+        preferred_element_type=jnp.float32,
+    )
+    rows = scaling * rows
     out_ref[...] = rows.astype(jnp.bfloat16)
 
 

time: 101 us -> 101 us (level)
  transfers between devices with their start and end apart: 12 -> 12, of which waited for: 6 -> 6; matrix products, arithmetic and copies ran while one was open for 0% -> 0% of each run, Pallas kernels for 3% -> 2%
where the time goes in v5:
time: 101 us
  starting transfers between devices  28.9 us (29%)
  waiting for transfers between devices  22.9 us (23%)
  blocking collectives  21.8 us (22%)
  between operations  13.5 us (13%)
  Pallas kernels  12.7 us (13%)
    ppermute x7, waiting for transfers between devices, next_dp(): return lax.ppermute(part, ('rep', 'dp'), round_dp)  22.2 us
    all_to_all x1, blocking collectives, body(): lax.all_to_all(grad_send, 'expert', split_axis=0, concat_axis=0, tiled=True)  21.8 us
    ppermute x7, starting transfers between devices, next_dp(): return lax.ppermute(part, ('rep', 'dp'), round_dp)  18.1 us
    ppermute x4, starting transfers between devices, other_core(): return lax.ppermute(part, 'rep', cores)  10.7 us
    pallas_call x1, Pallas kernels, product(): pl.pallas_call(product_kernel, grid=(width // tile,), in_specs=in_specs,...  10.4 us
    pallas_call x1, Pallas kernels, outgoing_rows(): pl.pallas_call(lambda *refs: rows_kernel(*refs, experts=experts_all, scal...  2.28 us
  transfers between devices with their start and end apart: 12, of which 6 were waited for; matrix products, arithmetic and copies ran while one was open for 0% of the time, Pallas kernels for 2%

profile of v5, /device:TPU:6, one launch (start us, length us, event | category | flops | bytes accessed | tf_op | source)
XLA Modules:
  0.0 100.5 jit_solution(1782059276542872925)
XLA Ops:
  6.5 0.0 all-gather.3.cloned.1.call-start
  6.5 0.7 all-gather.3.cloned.1.call-update
  7.3 2.3 %shard_map.73 = bf16[384,512]{1,0:T(8,128)(2,1)} custom-call(bf16[128,512]{1,0:T(8,128)(2,1)} %refs_0_.1, bf16[128,512]{1,0:T(8,128)(2,1)} %refs_1_.1, f32[1,512]{1,0:T(1,128)} %bitcast.14, s32[1,128]{1,0:T(1,128)} %bitcast.17, s32[2,128]{1,0:T(2,128)} %bitcast.15, f32[2,128]{1,0:T(2,128)} %bitcast.16), custom_call_target="tpu_custom_call" | custom-call | tf_op jit(solution)/shard_map/pallas_call | solution.py:52
  9.5 21.8 %all_to_all.5 = bf16[8,48,512]{2,1,0:T(8,128)(2,1)S(1)} all-to-all(bf16[8,48,512]{2,1,0:T(8,128)(2,1)} %bitcast.13), channel_id=1, replica_groups=mesh['rep'=8,'dp'=8,'expert'=8] {'expert'}, dimensions={0} | all-to-all | bytes 786432 | tf_op jit(solution)/shard_map/all_to_all | solution.py:107
  31.3 1.9 %collective-permute-start.3 = (bf16[384,512]{1,0:T(8,128)(2,1)S(1)}, bf16[384,512]{1,0:T(8,128)(2,1)S(1)}, u32[]{:S(2)}, u32[]{:S(2)}) collective-permute-start(bf16[384,512]{1,0:T(8,128)(2,1)S(1)} %bitcast.10), channel_id=1, source_target_pairs={{0,64},{64,0},{128,192},{192,128},{256,320},{320,256},{384,448},{4... | collective-permute-start | bytes 1179656 | tf_op jit(solution)/shard_map/ppermute | solution.py:116
  33.2 4.3 %collective-permute-start = (bf16[384,512]{1,0:T(8,128)(2,1)S(1)}, bf16[384,512]{1,0:T(8,128)(2,1)S(1)}, u32[]{:S(2)}, u32[]{:S(2)}) collective-permute-start(bf16[384,512]{1,0:T(8,128)(2,1)S(1)} %bitcast.11), channel_id=1, source_target_pairs={{0,8},{8,16},{16,24},{24,32},{32,40},{40,48},{48,56},{56,0},{64,12... | collective-permute-start | bytes 1179656 | tf_op jit(solution)/shard_map/ppermute | solution.py:113
  37.5 0.0 collective-permute-done.3
  37.5 4.3 %collective-permute-start.4 = (bf16[384,512]{1,0:T(8,128)(2,1)S(1)}, bf16[384,512]{1,0:T(8,128)(2,1)S(1)}, u32[]{:S(2)}, u32[]{:S(2)}) collective-permute-start(bf16[384,512]{1,0:T(8,128)(2,1)S(1)} %collective-permute-done.3), channel_id=1, source_target_pairs={{0,8},{8,16},{16,24},{24,32},{32,40},{40,48},{48,56},{56,0},{64,12... | collective-permute-start | bytes 1179656 | tf_op jit(solution)/shard_map/ppermute | solution.py:113
  41.8 8.1 %collective-permute-done.refs_1_ = bf16[384,512]{1,0:T(8,128)(2,1)S(1)} collective-permute-done((bf16[384,512]{1,0:T(8,128)(2,1)S(1)}, bf16[384,512]{1,0:T(8,128)(2,1)S(1)}, u32[]{:S(2)}, u32[]{:S(2)}) %collective-permute-start) | collective-permute-done | bytes 393248 | tf_op jit(solution)/shard_map/ppermute | solution.py:113
  49.9 1.9 %collective-permute-start.1 = (bf16[384,512]{1,0:T(8,128)(2,1)S(1)}, bf16[384,512]{1,0:T(8,128)(2,1)S(1)}, u32[]{:S(2)}, u32[]{:S(2)}) collective-permute-start(bf16[384,512]{1,0:T(8,128)(2,1)S(1)} %collective-permute-done.refs_1_), channel_id=1, source_target_pairs={{0,8},{8,16},{16,24},{24,32},{32,40},{40,48},{48,56},{56,0},{64,12... | collective-permute-start | bytes 1179656 | tf_op jit(solution)/shard_map/ppermute | solution.py:113
  51.9 2.3 %collective-permute-done.4 = bf16[384,512]{1,0:T(8,128)(2,1)S(1)} collective-permute-done((bf16[384,512]{1,0:T(8,128)(2,1)S(1)}, bf16[384,512]{1,0:T(8,128)(2,1)S(1)}, u32[]{:S(2)}, u32[]{:S(2)}) %collective-permute-start.4) | collective-permute-done | bytes 393248 | tf_op jit(solution)/shard_map/ppermute | solution.py:113
  54.2 1.9 %collective-permute-start.7 = (bf16[384,512]{1,0:T(8,128)(2,1)S(1)}, bf16[384,512]{1,0:T(8,128)(2,1)S(1)}, u32[]{:S(2)}, u32[]{:S(2)}) collective-permute-start(bf16[384,512]{1,0:T(8,128)(2,1)S(1)} %collective-permute-done.4), channel_id=1, source_target_pairs={{0,8},{8,16},{16,24},{24,32},{32,40},{40,48},{48,56},{56,0},{64,12... | collective-permute-start | bytes 1179656 | tf_op jit(solution)/shard_map/ppermute | solution.py:113
  56.1 4.7 %collective-permute-done.1.refs_2_ = bf16[384,512]{1,0:T(8,128)(2,1)S(1)} collective-permute-done((bf16[384,512]{1,0:T(8,128)(2,1)S(1)}, bf16[384,512]{1,0:T(8,128)(2,1)S(1)}, u32[]{:S(2)}, u32[]{:S(2)}) %collective-permute-start.1) | collective-permute-done | bytes 393248 | tf_op jit(solution)/shard_map/ppermute | solution.py:113
  60.8 1.9 %collective-permute-start.2 = (bf16[384,512]{1,0:T(8,128)(2,1)S(1)}, bf16[384,512]{1,0:T(8,128)(2,1)S(1)}, u32[]{:S(2)}, u32[]{:S(2)}) collective-permute-start(bf16[384,512]{1,0:T(8,128)(2,1)S(1)} %collective-permute-done.1.refs_2_), channel_id=1, source_target_pairs={{0,8},{8,16},{16,24},{24,32},{32,40},{40,48},{48,56},{56,0},{64,12... | collective-permute-start | bytes 1179656 | tf_op jit(solution)/shard_map/ppermute | solution.py:113
  62.7 3.8 %collective-permute-start.5 = (bf16[384,512]{1,0:T(8,128)(2,1)S(1)}, bf16[384,512]{1,0:T(8,128)(2,1)S(1)}, u32[]{:S(2)}, u32[]{:S(2)}) collective-permute-start(bf16[384,512]{1,0:T(8,128)(2,1)S(1)} %collective-permute-done.4), channel_id=1, source_target_pairs={{0,64},{64,0},{128,192},{192,128},{256,320},{320,256},{384,448},{4... | collective-permute-start | bytes 1179656 | tf_op jit(solution)/shard_map/ppermute | solution.py:116
  66.6 0.0 collective-permute-done.7
  66.6 1.9 %collective-permute-start.9 = (bf16[384,512]{1,0:T(8,128)(2,1)S(1)}, bf16[384,512]{1,0:T(8,128)(2,1)S(1)}, u32[]{:S(2)}, u32[]{:S(2)}) collective-permute-start(bf16[384,512]{1,0:T(8,128)(2,1)S(1)} %collective-permute-done.7), channel_id=1, source_target_pairs={{0,8},{8,16},{16,24},{24,32},{32,40},{40,48},{48,56},{56,0},{64,12... | collective-permute-start | bytes 1179656 | tf_op jit(solution)/shard_map/ppermute | solution.py:113
  68.5 3.2 %collective-permute-done.2.refs_3_ = bf16[384,512]{1,0:T(8,128)(2,1)S(1)} collective-permute-done((bf16[384,512]{1,0:T(8,128)(2,1)S(1)}, bf16[384,512]{1,0:T(8,128)(2,1)S(1)}, u32[]{:S(2)}, u32[]{:S(2)}) %collective-permute-start.2) | collective-permute-done | bytes 393248 | tf_op jit(solution)/shard_map/ppermute | solution.py:113
  71.7 0.0 collective-permute-done.5.refs_5_
  71.7 0.0 copy-start
  71.7 1.9 %collective-permute-start.6 = (bf16[384,512]{1,0:T(8,128)(2,1)S(1)}, bf16[384,512]{1,0:T(8,128)(2,1)S(1)}, u32[]{:S(2)}, u32[]{:S(2)}) collective-permute-start(bf16[384,512]{1,0:T(8,128)(2,1)S(1)} %collective-permute-done.2.refs_3_), channel_id=1, source_target_pairs={{0,8},{8,16},{16,24},{24,32},{32,40},{40,48},{48,56},{56,0},{64,12... | collective-permute-start | bytes 1179656 | tf_op jit(solution)/shard_map/ppermute | solution.py:113
  73.6 3.1 %collective-permute-start.8 = (bf16[384,512]{1,0:T(8,128)(2,1)S(1)}, bf16[384,512]{1,0:T(8,128)(2,1)S(1)}, u32[]{:S(2)}, u32[]{:S(2)}) collective-permute-start(bf16[384,512]{1,0:T(8,128)(2,1)S(1)} %collective-permute-done.7), channel_id=1, source_target_pairs={{0,64},{64,0},{128,192},{192,128},{256,320},{320,256},{384,448},{4... | collective-permute-start | bytes 1179656 | tf_op jit(solution)/shard_map/ppermute | solution.py:116
  76.7 0.8 collective-permute-done.9
  77.5 1.9 %collective-permute-start.10 = (bf16[384,512]{1,0:T(8,128)(2,1)S(1)}, bf16[384,512]{1,0:T(8,128)(2,1)}, u32[]{:S(2)}, u32[]{:S(2)}) collective-permute-start(bf16[384,512]{1,0:T(8,128)(2,1)S(1)} %collective-permute-done.9), channel_id=1, source_target_pairs={{0,64},{64,0},{128,192},{192,128},{256,320},{320,256},{384,448},{4... | collective-permute-start | bytes 1179656 | tf_op jit(solution)/shard_map/ppermute | solution.py:116
  79.4 0.1 pad_add_fusion.place_ref
  79.5 3.1 %collective-permute-done.6.refs_4_ = bf16[384,512]{1,0:T(8,128)(2,1)S(1)} collective-permute-done((bf16[384,512]{1,0:T(8,128)(2,1)S(1)}, bf16[384,512]{1,0:T(8,128)(2,1)S(1)}, u32[]{:S(2)}, u32[]{:S(2)}) %collective-permute-start.6) | collective-permute-done | bytes 393248 | tf_op jit(solution)/shard_map/ppermute | solution.py:113
  82.6 0.0 collective-permute-done.8.refs_6_
  82.6 0.0 copy-start.1
  82.6 0.0 collective-permute-done.10.refs_7_
  82.6 0.0 all-gather.3.cloned.1.call-done
  82.6 0.0 copy-done
  82.6 0.7 copy-done.1
  83.3 10.4 %shard_map.74 = f32[1792,512]{1,0:T(8,128)} custom-call(s32[2]{0:T(128)S(1)} %pad_add_fusion.place_ref, bf16[3072,1792]{1,0:T(8,128)(2,1)} %bitcast.18, bf16[384,512]{1,0:T(8,128)(2,1)S(1)} %bitcast.12, bf16[384,512]{1,0:T(8,128)(2,1)S(1)} %collective-permute-done.refs_1_, bf16[384,512]{1,0:T(8,128)(2,1)S(1)} %collective-permute-done.1.refs_2_, ...), custom_call_target="tpu_custom_call" | custom-call | flops 5637144576 | bytes 17825792 | tf_op jit(solution)/shard_map/pallas_call | solution.py:83
Async XLA Ops:
  6.5 76.1 %all-gather.3.cloned.1.call-start = ((), (), s32[]{:S(2)}) async-start(), calls=%async_computation.1 | async-start | bytes 12386304 | tf_op jit(solution)/shard_map/all_gather | solution.py:106
  31.3 6.2 %collective-permute-start.3 = (bf16[384,512]{1,0:T(8,128)(2,1)S(1)}, bf16[384,512]{1,0:T(8,128)(2,1)S(1)}, u32[]{:S(2)}, u32[]{:S(2)}) collective-permute-start(bf16[384,512]{1,0:T(8,128)(2,1)S(1)} %bitcast.10), channel_id=1, source_target_pairs={{0,64},{64,0},{128,192},{192,128},{256,320},{320,256},{384,448},{4... | collective-permute-start | bytes 1179656 | tf_op jit(solution)/shard_map/ppermute | solution.py:116
  33.2 16.7 %collective-permute-start = (bf16[384,512]{1,0:T(8,128)(2,1)S(1)}, bf16[384,512]{1,0:T(8,128)(2,1)S(1)}, u32[]{:S(2)}, u32[]{:S(2)}) collective-permute-start(bf16[384,512]{1,0:T(8,128)(2,1)S(1)} %bitcast.11), channel_id=1, source_target_pairs={{0,8},{8,16},{16,24},{24,32},{32,40},{40,48},{48,56},{56,0},{64,12... | collective-permute-start | bytes 1179656 | tf_op jit(solution)/shard_map/ppermute | solution.py:113
  37.5 16.6 %collective-permute-start.4 = (bf16[384,512]{1,0:T(8,128)(2,1)S(1)}, bf16[384,512]{1,0:T(8,128)(2,1)S(1)}, u32[]{:S(2)}, u32[]{:S(2)}) collective-permute-start(bf16[384,512]{1,0:T(8,128)(2,1)S(1)} %collective-permute-done.3), channel_id=1, source_target_pairs={{0,8},{8,16},{16,24},{24,32},{32,40},{40,48},{48,56},{56,0},{64,12... | collective-permute-start | bytes 1179656 | tf_op jit(solution)/shard_map/ppermute | solution.py:113
  49.9 10.9 %collective-permute-start.1 = (bf16[384,512]{1,0:T(8,128)(2,1)S(1)}, bf16[384,512]{1,0:T(8,128)(2,1)S(1)}, u32[]{:S(2)}, u32[]{:S(2)}) collective-permute-start(bf16[384,512]{1,0:T(8,128)(2,1)S(1)} %collective-permute-done.refs_1_), channel_id=1, source_target_pairs={{0,8},{8,16},{16,24},{24,32},{32,40},{40,48},{48,56},{56,0},{64,12... | collective-permute-start | bytes 1179656 | tf_op jit(solution)/shard_map/ppermute | solution.py:113
  54.2 12.4 %collective-permute-start.7 = (bf16[384,512]{1,0:T(8,128)(2,1)S(1)}, bf16[384,512]{1,0:T(8,128)(2,1)S(1)}, u32[]{:S(2)}, u32[]{:S(2)}) collective-permute-start(bf16[384,512]{1,0:T(8,128)(2,1)S(1)} %collective-permute-done.4), channel_id=1, source_target_pairs={{0,8},{8,16},{16,24},{24,32},{32,40},{40,48},{48,56},{56,0},{64,12... | collective-permute-start | bytes 1179656 | tf_op jit(solution)/shard_map/ppermute | solution.py:113
  60.8 10.9 %collective-permute-start.2 = (bf16[384,512]{1,0:T(8,128)(2,1)S(1)}, bf16[384,512]{1,0:T(8,128)(2,1)S(1)}, u32[]{:S(2)}, u32[]{:S(2)}) collective-permute-start(bf16[384,512]{1,0:T(8,128)(2,1)S(1)} %collective-permute-done.1.refs_2_), channel_id=1, source_target_pairs={{0,8},{8,16},{16,24},{24,32},{32,40},{40,48},{48,56},{56,0},{64,12... | collective-permute-start | bytes 1179656 | tf_op jit(solution)/shard_map/ppermute | solution.py:113
  62.7 9.0 %collective-permute-start.5 = (bf16[384,512]{1,0:T(8,128)(2,1)S(1)}, bf16[384,512]{1,0:T(8,128)(2,1)S(1)}, u32[]{:S(2)}, u32[]{:S(2)}) collective-permute-start(bf16[384,512]{1,0:T(8,128)(2,1)S(1)} %collective-permute-done.4), channel_id=1, source_target_pairs={{0,64},{64,0},{128,192},{192,128},{256,320},{320,256},{384,448},{4... | collective-permute-start | bytes 1179656 | tf_op jit(solution)/shard_map/ppermute | solution.py:116
  66.6 10.9 %collective-permute-start.9 = (bf16[384,512]{1,0:T(8,128)(2,1)S(1)}, bf16[384,512]{1,0:T(8,128)(2,1)S(1)}, u32[]{:S(2)}, u32[]{:S(2)}) collective-permute-start(bf16[384,512]{1,0:T(8,128)(2,1)S(1)} %collective-permute-done.7), channel_id=1, source_target_pairs={{0,8},{8,16},{16,24},{24,32},{32,40},{40,48},{48,56},{56,0},{64,12... | collective-permute-start | bytes 1179656 | tf_op jit(solution)/shard_map/ppermute | solution.py:113
  71.7 10.9 %copy-start = (bf16[384,512]{1,0:T(8,128)(2,1)}, bf16[384,512]{1,0:T(8,128)(2,1)S(1)}, u32[]{:S(2)}) copy-start(bf16[384,512]{1,0:T(8,128)(2,1)S(1)} %collective-permute-done.5.refs_5_) | copy-start | bytes 1179652
  71.7 10.9 %collective-permute-start.6 = (bf16[384,512]{1,0:T(8,128)(2,1)S(1)}, bf16[384,512]{1,0:T(8,128)(2,1)S(1)}, u32[]{:S(2)}, u32[]{:S(2)}) collective-permute-start(bf16[384,512]{1,0:T(8,128)(2,1)S(1)} %collective-permute-done.2.refs_3_), channel_id=1, source_target_pairs={{0,8},{8,16},{16,24},{24,32},{32,40},{40,48},{48,56},{56,0},{64,12... | collective-permute-start | bytes 1179656 | tf_op jit(solution)/shard_map/ppermute | solution.py:113
  73.6 9.0 %collective-permute-start.8 = (bf16[384,512]{1,0:T(8,128)(2,1)S(1)}, bf16[384,512]{1,0:T(8,128)(2,1)S(1)}, u32[]{:S(2)}, u32[]{:S(2)}) collective-permute-start(bf16[384,512]{1,0:T(8,128)(2,1)S(1)} %collective-permute-done.7), channel_id=1, source_target_pairs={{0,64},{64,0},{128,192},{192,128},{256,320},{320,256},{384,448},{4... | collective-permute-start | bytes 1179656 | tf_op jit(solution)/shard_map/ppermute | solution.py:116
  77.5 5.1 %collective-permute-start.10 = (bf16[384,512]{1,0:T(8,128)(2,1)S(1)}, bf16[384,512]{1,0:T(8,128)(2,1)}, u32[]{:S(2)}, u32[]{:S(2)}) collective-permute-start(bf16[384,512]{1,0:T(8,128)(2,1)S(1)} %collective-permute-done.9), channel_id=1, source_target_pairs={{0,64},{64,0},{128,192},{192,128},{256,320},{320,256},{384,448},{4... | collective-permute-start | bytes 1179656 | tf_op jit(solution)/shard_map/ppermute | solution.py:116
  82.6 0.7 copy-start.1
Sparse Core Ops, SparseCore 0:
  9.5 69.2 all-gather.2

commit v6 on v5

--- a/solution.py
+++ b/solution.py
@@ -58,19 +58,19 @@
 
 
 def product_kernel(place_ref, slots, *refs):
-    pieces, (out_ref, rows) = refs[:-2], refs[-2:]
+    pieces, out_ref = refs[:-1], refs[-1]
     block = pieces[0].shape[0]
-
-    @pl.when(pl.program_id(0) == 0)
-    def _():
-        rep, dp = place_ref[0], place_ref[1]
-        way = jnp.where(lax.rem(rep, 2) == 0, -1, 1)
-        for piece, hops in zip(pieces, (0, 1, 2, 3, 4, -1, -2, -3)):
-            slot_block = lax.rem(dp + way * hops + 8, 8)
-            rows[pl.ds(pl.multiple_of(slot_block * block, block), block), :] = piece[...]
-
+    rep, dp = place_ref[0], place_ref[1]
+    way = jnp.where(lax.rem(rep, 2) == 0, -1, 1)
+    held = []
+    for hops in (0, 1, 2, 3, 4, -1, -2, -3):
+        slot_block = lax.rem(dp + way * hops + 8, 8)
+        held.append(slots[pl.ds(pl.multiple_of(slot_block * block, block), block), :])
     out_ref[...] = lax.dot_general(
-        slots[...], rows[...], (((0,), (0,)), ((), ())), preferred_element_type=jnp.float32
+        jnp.concatenate(held, axis=0),
+        jnp.concatenate([piece[...] for piece in pieces], axis=0),
+        (((0,), (0,)), ((), ())),
+        preferred_element_type=jnp.float32,
     )
 
 
@@ -86,7 +86,6 @@
         in_specs=in_specs,
         out_specs=pl.BlockSpec((tile, cols), lambda i: (i, 0)),
         out_shape=jax.ShapeDtypeStruct((width, cols), jnp.float32),
-        scratch_shapes=[pltpu.VMEM((8 * block, cols), jnp.bfloat16)],
         compiler_params=pltpu.CompilerParams(vmem_limit_bytes=52 * 2**20),
         cost_estimate=pl.CostEstimate(
             flops=2 * 8 * block * cols * width, bytes_accessed=8 * block * (cols + width) * 2 + width * cols * 4, transcendentals=0

time: 101 us -> 101 us (level)
  no operation moved by 1% of the time
where the time goes in v6:
time: 101 us; the launch traced here: 100 us
  starting transfers between devices  28.9 us (29%)
  waiting for transfers between devices  22.9 us (23%)
  blocking collectives  21.8 us (22%)
  between operations  13.5 us (13%)
  Pallas kernels  12.5 us (12%)
    ppermute x7, waiting for transfers between devices, next_dp(): return lax.ppermute(part, ('rep', 'dp'), round_dp)  22.2 us
    all_to_all x1, blocking collectives, body(): lax.all_to_all(grad_send, 'expert', split_axis=0, concat_axis=0, tiled=True)  21.8 us
    ppermute x7, starting transfers between devices, next_dp(): return lax.ppermute(part, ('rep', 'dp'), round_dp)  18.1 us
    ppermute x4, starting transfers between devices, other_core(): return lax.ppermute(part, 'rep', cores)  10.7 us
    pallas_call x1, Pallas kernels, product(): pl.pallas_call(product_kernel, grid=(width // tile,), in_specs=in_specs,...  10.2 us
    pallas_call x1, Pallas kernels, outgoing_rows(): pl.pallas_call(lambda *refs: rows_kernel(*refs, experts=experts_all, scal...  2.28 us
  transfers between devices with their start and end apart: 12, of which 6 were waited for; matrix products, arithmetic and copies ran while one was open for 0% of the time, Pallas kernels for 2%

profile of v6, /device:TPU:6, one launch (start us, length us, event | category | flops | bytes accessed | tf_op | source)
XLA Modules:
  0.0 100.3 jit_solution(3333103801732564644)
XLA Ops:
  6.5 0.0 all-gather.3.cloned.1.call-start
  6.5 0.7 all-gather.3.cloned.1.call-update
  7.3 2.3 %shard_map.73 = bf16[384,512]{1,0:T(8,128)(2,1)} custom-call(bf16[128,512]{1,0:T(8,128)(2,1)} %refs_0_.1, bf16[128,512]{1,0:T(8,128)(2,1)} %refs_1_.1, f32[1,512]{1,0:T(1,128)} %bitcast.14, s32[1,128]{1,0:T(1,128)} %bitcast.17, s32[2,128]{1,0:T(2,128)} %bitcast.15, f32[2,128]{1,0:T(2,128)} %bitcast.16), custom_call_target="tpu_custom_call" | custom-call | tf_op jit(solution)/shard_map/pallas_call | solution.py:52
  9.5 21.8 %all_to_all.5 = bf16[8,48,512]{2,1,0:T(8,128)(2,1)S(1)} all-to-all(bf16[8,48,512]{2,1,0:T(8,128)(2,1)} %bitcast.13), channel_id=1, replica_groups=mesh['rep'=8,'dp'=8,'expert'=8] {'expert'}, dimensions={0} | all-to-all | bytes 786432 | tf_op jit(solution)/shard_map/all_to_all | solution.py:106
  31.3 1.9 %collective-permute-start.3 = (bf16[384,512]{1,0:T(8,128)(2,1)S(1)}, bf16[384,512]{1,0:T(8,128)(2,1)S(1)}, u32[]{:S(2)}, u32[]{:S(2)}) collective-permute-start(bf16[384,512]{1,0:T(8,128)(2,1)S(1)} %bitcast.10), channel_id=1, source_target_pairs={{0,64},{64,0},{128,192},{192,128},{256,320},{320,256},{384,448},{4... | collective-permute-start | bytes 1179656 | tf_op jit(solution)/shard_map/ppermute | solution.py:115
  33.2 4.3 %collective-permute-start = (bf16[384,512]{1,0:T(8,128)(2,1)S(1)}, bf16[384,512]{1,0:T(8,128)(2,1)S(1)}, u32[]{:S(2)}, u32[]{:S(2)}) collective-permute-start(bf16[384,512]{1,0:T(8,128)(2,1)S(1)} %bitcast.11), channel_id=1, source_target_pairs={{0,8},{8,16},{16,24},{24,32},{32,40},{40,48},{48,56},{56,0},{64,12... | collective-permute-start | bytes 1179656 | tf_op jit(solution)/shard_map/ppermute | solution.py:112
  37.5 0.0 collective-permute-done.3
  37.5 4.3 %collective-permute-start.4 = (bf16[384,512]{1,0:T(8,128)(2,1)S(1)}, bf16[384,512]{1,0:T(8,128)(2,1)S(1)}, u32[]{:S(2)}, u32[]{:S(2)}) collective-permute-start(bf16[384,512]{1,0:T(8,128)(2,1)S(1)} %collective-permute-done.3), channel_id=1, source_target_pairs={{0,8},{8,16},{16,24},{24,32},{32,40},{40,48},{48,56},{56,0},{64,12... | collective-permute-start | bytes 1179656 | tf_op jit(solution)/shard_map/ppermute | solution.py:112
  41.8 8.1 %collective-permute-done.refs_1_ = bf16[384,512]{1,0:T(8,128)(2,1)S(1)} collective-permute-done((bf16[384,512]{1,0:T(8,128)(2,1)S(1)}, bf16[384,512]{1,0:T(8,128)(2,1)S(1)}, u32[]{:S(2)}, u32[]{:S(2)}) %collective-permute-start) | collective-permute-done | bytes 393248 | tf_op jit(solution)/shard_map/ppermute | solution.py:112
  49.9 1.9 %collective-permute-start.1 = (bf16[384,512]{1,0:T(8,128)(2,1)S(1)}, bf16[384,512]{1,0:T(8,128)(2,1)S(1)}, u32[]{:S(2)}, u32[]{:S(2)}) collective-permute-start(bf16[384,512]{1,0:T(8,128)(2,1)S(1)} %collective-permute-done.refs_1_), channel_id=1, source_target_pairs={{0,8},{8,16},{16,24},{24,32},{32,40},{40,48},{48,56},{56,0},{64,12... | collective-permute-start | bytes 1179656 | tf_op jit(solution)/shard_map/ppermute | solution.py:112
  51.9 2.3 %collective-permute-done.4 = bf16[384,512]{1,0:T(8,128)(2,1)S(1)} collective-permute-done((bf16[384,512]{1,0:T(8,128)(2,1)S(1)}, bf16[384,512]{1,0:T(8,128)(2,1)S(1)}, u32[]{:S(2)}, u32[]{:S(2)}) %collective-permute-start.4) | collective-permute-done | bytes 393248 | tf_op jit(solution)/shard_map/ppermute | solution.py:112
  54.2 1.9 %collective-permute-start.7 = (bf16[384,512]{1,0:T(8,128)(2,1)S(1)}, bf16[384,512]{1,0:T(8,128)(2,1)S(1)}, u32[]{:S(2)}, u32[]{:S(2)}) collective-permute-start(bf16[384,512]{1,0:T(8,128)(2,1)S(1)} %collective-permute-done.4), channel_id=1, source_target_pairs={{0,8},{8,16},{16,24},{24,32},{32,40},{40,48},{48,56},{56,0},{64,12... | collective-permute-start | bytes 1179656 | tf_op jit(solution)/shard_map/ppermute | solution.py:112
  56.1 4.7 %collective-permute-done.1.refs_2_ = bf16[384,512]{1,0:T(8,128)(2,1)S(1)} collective-permute-done((bf16[384,512]{1,0:T(8,128)(2,1)S(1)}, bf16[384,512]{1,0:T(8,128)(2,1)S(1)}, u32[]{:S(2)}, u32[]{:S(2)}) %collective-permute-start.1) | collective-permute-done | bytes 393248 | tf_op jit(solution)/shard_map/ppermute | solution.py:112
  60.8 1.9 %collective-permute-start.2 = (bf16[384,512]{1,0:T(8,128)(2,1)S(1)}, bf16[384,512]{1,0:T(8,128)(2,1)S(1)}, u32[]{:S(2)}, u32[]{:S(2)}) collective-permute-start(bf16[384,512]{1,0:T(8,128)(2,1)S(1)} %collective-permute-done.1.refs_2_), channel_id=1, source_target_pairs={{0,8},{8,16},{16,24},{24,32},{32,40},{40,48},{48,56},{56,0},{64,12... | collective-permute-start | bytes 1179656 | tf_op jit(solution)/shard_map/ppermute | solution.py:112
  62.7 3.8 %collective-permute-start.5 = (bf16[384,512]{1,0:T(8,128)(2,1)S(1)}, bf16[384,512]{1,0:T(8,128)(2,1)S(1)}, u32[]{:S(2)}, u32[]{:S(2)}) collective-permute-start(bf16[384,512]{1,0:T(8,128)(2,1)S(1)} %collective-permute-done.4), channel_id=1, source_target_pairs={{0,64},{64,0},{128,192},{192,128},{256,320},{320,256},{384,448},{4... | collective-permute-start | bytes 1179656 | tf_op jit(solution)/shard_map/ppermute | solution.py:115
  66.6 0.0 collective-permute-done.7
  66.6 1.9 %collective-permute-start.9 = (bf16[384,512]{1,0:T(8,128)(2,1)S(1)}, bf16[384,512]{1,0:T(8,128)(2,1)S(1)}, u32[]{:S(2)}, u32[]{:S(2)}) collective-permute-start(bf16[384,512]{1,0:T(8,128)(2,1)S(1)} %collective-permute-done.7), channel_id=1, source_target_pairs={{0,8},{8,16},{16,24},{24,32},{32,40},{40,48},{48,56},{56,0},{64,12... | collective-permute-start | bytes 1179656 | tf_op jit(solution)/shard_map/ppermute | solution.py:112
  68.5 3.2 %collective-permute-done.2.refs_3_ = bf16[384,512]{1,0:T(8,128)(2,1)S(1)} collective-permute-done((bf16[384,512]{1,0:T(8,128)(2,1)S(1)}, bf16[384,512]{1,0:T(8,128)(2,1)S(1)}, u32[]{:S(2)}, u32[]{:S(2)}) %collective-permute-start.2) | collective-permute-done | bytes 393248 | tf_op jit(solution)/shard_map/ppermute | solution.py:112
  71.7 0.0 collective-permute-done.5.refs_5_
  71.7 0.0 copy-start
  71.7 1.9 %collective-permute-start.6 = (bf16[384,512]{1,0:T(8,128)(2,1)S(1)}, bf16[384,512]{1,0:T(8,128)(2,1)S(1)}, u32[]{:S(2)}, u32[]{:S(2)}) collective-permute-start(bf16[384,512]{1,0:T(8,128)(2,1)S(1)} %collective-permute-done.2.refs_3_), channel_id=1, source_target_pairs={{0,8},{8,16},{16,24},{24,32},{32,40},{40,48},{48,56},{56,0},{64,12... | collective-permute-start | bytes 1179656 | tf_op jit(solution)/shard_map/ppermute | solution.py:112
  73.6 3.1 %collective-permute-start.8 = (bf16[384,512]{1,0:T(8,128)(2,1)S(1)}, bf16[384,512]{1,0:T(8,128)(2,1)S(1)}, u32[]{:S(2)}, u32[]{:S(2)}) collective-permute-start(bf16[384,512]{1,0:T(8,128)(2,1)S(1)} %collective-permute-done.7), channel_id=1, source_target_pairs={{0,64},{64,0},{128,192},{192,128},{256,320},{320,256},{384,448},{4... | collective-permute-start | bytes 1179656 | tf_op jit(solution)/shard_map/ppermute | solution.py:115
  76.7 0.8 collective-permute-done.9
  77.5 1.9 %collective-permute-start.10 = (bf16[384,512]{1,0:T(8,128)(2,1)S(1)}, bf16[384,512]{1,0:T(8,128)(2,1)}, u32[]{:S(2)}, u32[]{:S(2)}) collective-permute-start(bf16[384,512]{1,0:T(8,128)(2,1)S(1)} %collective-permute-done.9), channel_id=1, source_target_pairs={{0,64},{64,0},{128,192},{192,128},{256,320},{320,256},{384,448},{4... | collective-permute-start | bytes 1179656 | tf_op jit(solution)/shard_map/ppermute | solution.py:115
  79.4 0.1 pad_add_fusion.place_ref
  79.5 3.1 %collective-permute-done.6.refs_4_ = bf16[384,512]{1,0:T(8,128)(2,1)S(1)} collective-permute-done((bf16[384,512]{1,0:T(8,128)(2,1)S(1)}, bf16[384,512]{1,0:T(8,128)(2,1)S(1)}, u32[]{:S(2)}, u32[]{:S(2)}) %collective-permute-start.6) | collective-permute-done | bytes 393248 | tf_op jit(solution)/shard_map/ppermute | solution.py:112
  82.6 0.0 collective-permute-done.8.refs_6_
  82.6 0.0 copy-start.1
  82.6 0.0 collective-permute-done.10.refs_7_
  82.6 0.0 all-gather.3.cloned.1.call-done
  82.6 0.0 copy-done
  82.6 0.7 copy-done.1
  83.3 10.2 %shard_map.74 = f32[1792,512]{1,0:T(8,128)} custom-call(s32[2]{0:T(128)S(1)} %pad_add_fusion.place_ref, bf16[3072,1792]{1,0:T(8,128)(2,1)} %bitcast.18, bf16[384,512]{1,0:T(8,128)(2,1)S(1)} %bitcast.12, bf16[384,512]{1,0:T(8,128)(2,1)S(1)} %collective-permute-done.refs_1_, bf16[384,512]{1,0:T(8,128)(2,1)S(1)} %collective-permute-done.1.refs_2_, ...), custom_call_target="tpu_custom_call" | custom-call | flops 5637144576 | bytes 17825792 | tf_op jit(solution)/shard_map/pallas_call | solution.py:83
Async XLA Ops:
  6.5 76.1 %all-gather.3.cloned.1.call-start = ((), (), s32[]{:S(2)}) async-start(), calls=%async_computation.1 | async-start | bytes 12386304 | tf_op jit(solution)/shard_map/all_gather | solution.py:105
  31.3 6.2 %collective-permute-start.3 = (bf16[384,512]{1,0:T(8,128)(2,1)S(1)}, bf16[384,512]{1,0:T(8,128)(2,1)S(1)}, u32[]{:S(2)}, u32[]{:S(2)}) collective-permute-start(bf16[384,512]{1,0:T(8,128)(2,1)S(1)} %bitcast.10), channel_id=1, source_target_pairs={{0,64},{64,0},{128,192},{192,128},{256,320},{320,256},{384,448},{4... | collective-permute-start | bytes 1179656 | tf_op jit(solution)/shard_map/ppermute | solution.py:115
  33.2 16.7 %collective-permute-start = (bf16[384,512]{1,0:T(8,128)(2,1)S(1)}, bf16[384,512]{1,0:T(8,128)(2,1)S(1)}, u32[]{:S(2)}, u32[]{:S(2)}) collective-permute-start(bf16[384,512]{1,0:T(8,128)(2,1)S(1)} %bitcast.11), channel_id=1, source_target_pairs={{0,8},{8,16},{16,24},{24,32},{32,40},{40,48},{48,56},{56,0},{64,12... | collective-permute-start | bytes 1179656 | tf_op jit(solution)/shard_map/ppermute | solution.py:112
  37.5 16.6 %collective-permute-start.4 = (bf16[384,512]{1,0:T(8,128)(2,1)S(1)}, bf16[384,512]{1,0:T(8,128)(2,1)S(1)}, u32[]{:S(2)}, u32[]{:S(2)}) collective-permute-start(bf16[384,512]{1,0:T(8,128)(2,1)S(1)} %collective-permute-done.3), channel_id=1, source_target_pairs={{0,8},{8,16},{16,24},{24,32},{32,40},{40,48},{48,56},{56,0},{64,12... | collective-permute-start | bytes 1179656 | tf_op jit(solution)/shard_map/ppermute | solution.py:112
  49.9 10.9 %collective-permute-start.1 = (bf16[384,512]{1,0:T(8,128)(2,1)S(1)}, bf16[384,512]{1,0:T(8,128)(2,1)S(1)}, u32[]{:S(2)}, u32[]{:S(2)}) collective-permute-start(bf16[384,512]{1,0:T(8,128)(2,1)S(1)} %collective-permute-done.refs_1_), channel_id=1, source_target_pairs={{0,8},{8,16},{16,24},{24,32},{32,40},{40,48},{48,56},{56,0},{64,12... | collective-permute-start | bytes 1179656 | tf_op jit(solution)/shard_map/ppermute | solution.py:112
  54.2 12.4 %collective-permute-start.7 = (bf16[384,512]{1,0:T(8,128)(2,1)S(1)}, bf16[384,512]{1,0:T(8,128)(2,1)S(1)}, u32[]{:S(2)}, u32[]{:S(2)}) collective-permute-start(bf16[384,512]{1,0:T(8,128)(2,1)S(1)} %collective-permute-done.4), channel_id=1, source_target_pairs={{0,8},{8,16},{16,24},{24,32},{32,40},{40,48},{48,56},{56,0},{64,12... | collective-permute-start | bytes 1179656 | tf_op jit(solution)/shard_map/ppermute | solution.py:112
  60.8 10.9 %collective-permute-start.2 = (bf16[384,512]{1,0:T(8,128)(2,1)S(1)}, bf16[384,512]{1,0:T(8,128)(2,1)S(1)}, u32[]{:S(2)}, u32[]{:S(2)}) collective-permute-start(bf16[384,512]{1,0:T(8,128)(2,1)S(1)} %collective-permute-done.1.refs_2_), channel_id=1, source_target_pairs={{0,8},{8,16},{16,24},{24,32},{32,40},{40,48},{48,56},{56,0},{64,12... | collective-permute-start | bytes 1179656 | tf_op jit(solution)/shard_map/ppermute | solution.py:112
  62.7 9.0 %collective-permute-start.5 = (bf16[384,512]{1,0:T(8,128)(2,1)S(1)}, bf16[384,512]{1,0:T(8,128)(2,1)S(1)}, u32[]{:S(2)}, u32[]{:S(2)}) collective-permute-start(bf16[384,512]{1,0:T(8,128)(2,1)S(1)} %collective-permute-done.4), channel_id=1, source_target_pairs={{0,64},{64,0},{128,192},{192,128},{256,320},{320,256},{384,448},{4... | collective-permute-start | bytes 1179656 | tf_op jit(solution)/shard_map/ppermute | solution.py:115
  66.6 10.9 %collective-permute-start.9 = (bf16[384,512]{1,0:T(8,128)(2,1)S(1)}, bf16[384,512]{1,0:T(8,128)(2,1)S(1)}, u32[]{:S(2)}, u32[]{:S(2)}) collective-permute-start(bf16[384,512]{1,0:T(8,128)(2,1)S(1)} %collective-permute-done.7), channel_id=1, source_target_pairs={{0,8},{8,16},{16,24},{24,32},{32,40},{40,48},{48,56},{56,0},{64,12... | collective-permute-start | bytes 1179656 | tf_op jit(solution)/shard_map/ppermute | solution.py:112
  71.7 10.9 %copy-start = (bf16[384,512]{1,0:T(8,128)(2,1)}, bf16[384,512]{1,0:T(8,128)(2,1)S(1)}, u32[]{:S(2)}) copy-start(bf16[384,512]{1,0:T(8,128)(2,1)S(1)} %collective-permute-done.5.refs_5_) | copy-start | bytes 1179652
  71.7 10.9 %collective-permute-start.6 = (bf16[384,512]{1,0:T(8,128)(2,1)S(1)}, bf16[384,512]{1,0:T(8,128)(2,1)S(1)}, u32[]{:S(2)}, u32[]{:S(2)}) collective-permute-start(bf16[384,512]{1,0:T(8,128)(2,1)S(1)} %collective-permute-done.2.refs_3_), channel_id=1, source_target_pairs={{0,8},{8,16},{16,24},{24,32},{32,40},{40,48},{48,56},{56,0},{64,12... | collective-permute-start | bytes 1179656 | tf_op jit(solution)/shard_map/ppermute | solution.py:112
  73.6 9.0 %collective-permute-start.8 = (bf16[384,512]{1,0:T(8,128)(2,1)S(1)}, bf16[384,512]{1,0:T(8,128)(2,1)S(1)}, u32[]{:S(2)}, u32[]{:S(2)}) collective-permute-start(bf16[384,512]{1,0:T(8,128)(2,1)S(1)} %collective-permute-done.7), channel_id=1, source_target_pairs={{0,64},{64,0},{128,192},{192,128},{256,320},{320,256},{384,448},{4... | collective-permute-start | bytes 1179656 | tf_op jit(solution)/shard_map/ppermute | solution.py:115
  77.5 5.1 %collective-permute-start.10 = (bf16[384,512]{1,0:T(8,128)(2,1)S(1)}, bf16[384,512]{1,0:T(8,128)(2,1)}, u32[]{:S(2)}, u32[]{:S(2)}) collective-permute-start(bf16[384,512]{1,0:T(8,128)(2,1)S(1)} %collective-permute-done.9), channel_id=1, source_target_pairs={{0,64},{64,0},{128,192},{192,128},{256,320},{320,256},{384,448},{4... | collective-permute-start | bytes 1179656 | tf_op jit(solution)/shard_map/ppermute | solution.py:115
  82.6 0.7 copy-start.1
Sparse Core Ops, SparseCore 0:
  9.5 69.2 all-gather.2
